TPU v7x, 128 devices: a whole 4x4x4 slice. The times are simulated.
128 devices in a mesh: dp: 8 (over y, x_lo), ctx: 16 (over x_hi, z, core).
Axes of the slice: x: 4 (x_hi: 2, x_lo: 2; x = x_hi * 2 + x_lo), y: 4, z: 4, core: 2. Of those that a mesh axis runs over, the one named last changes fastest.
Arguments:
- queries: bfloat16 [32768, 1024], P(('dp', 'ctx')), parts along dimension 0, may hold values from -6 to 6
- keys: bfloat16 [32768, 1024], P(('dp', 'ctx')), parts along dimension 0, may hold values from -6 to 6
- values: bfloat16 [32768, 1024], P(('dp', 'ctx')), parts along dimension 0, may hold values from -6 to 6
- grad_out: bfloat16 [32768, 1024], P(('dp', 'ctx')), parts along dimension 0, may hold values from -6 to 6
Outputs:
- attended: bfloat16 [32768, 1024], P(('dp', 'ctx')), parts along dimension 0
- query_grads: bfloat16 [32768, 1024], P(('dp', 'ctx')), parts along dimension 0
- key_grads: bfloat16 [32768, 1024], P(('dp', 'ctx')), parts along dimension 0
- value_grads: bfloat16 [32768, 1024], P(('dp', 'ctx')), parts along dimension 0
There are 8 independent parts, one for each index of `dp`. A program takes and returns all parts, laid end to end along the dimension named above; each array names one. Nothing has to cross between parts.
All inputs are finite; a program needn't handle non-finite values.
Results may differ from a plain program's by a relative error of at most 0.025.
Values may be sent and summed in bfloat16 or wider, within the bound.
No kernel may reach another device: no remote copies, remote signals or barrier semaphores. Data moves between devices by JAX's collectives and lax.ppermute only.
A program may use at most 192 MiB of HBM per device.

v0:
```python
import jax
import jax.numpy as jnp
from jax import lax
from jax.sharding import PartitionSpec as P

HEAD = 128
HEADS = 8


def on_device(queries, keys, values, grad_out):
    local_rows = queries.shape[0]
    softmax_scale = HEAD ** (-0.5)
    query_heads = queries.reshape(local_rows, HEADS, HEAD)
    cotangent = grad_out.reshape(local_rows, HEADS, HEAD)
    all_keys, all_values = (
        lax.all_gather(keys, "ctx", axis=0, tiled=True),
        lax.all_gather(values, "ctx", axis=0, tiled=True),
    )
    all_rows = all_keys.shape[0]
    key_heads = all_keys.reshape(all_rows, HEADS, HEAD)
    value_heads = all_values.reshape(all_rows, HEADS, HEAD)
    scores = (
        jnp.einsum("qhd,khd->hqk", query_heads, key_heads, preferred_element_type=jnp.float32)
        * softmax_scale
    )
    row_max = jnp.max(scores, axis=2, keepdims=True)
    log_total = row_max + jnp.log(jnp.sum(jnp.exp(scores - row_max), axis=2, keepdims=True))
    weights = jnp.exp(scores - log_total).astype(jnp.bfloat16)
    attended = jnp.einsum(
        "hqk,khd->qhd", weights, value_heads, preferred_element_type=jnp.float32
    ).astype(jnp.bfloat16)
    row_dots = jnp.sum(cotangent.astype(jnp.float32) * attended.astype(jnp.float32), axis=2)
    weight_grads = jnp.einsum(
        "qhd,khd->hqk", cotangent, value_heads, preferred_element_type=jnp.float32
    )
    score_grads = (weights.astype(jnp.float32) * (weight_grads - row_dots.T[:, :, None])).astype(
        jnp.bfloat16
    )
    query_grads = (
        softmax_scale
        * jnp.einsum("hqk,khd->qhd", score_grads, key_heads, preferred_element_type=jnp.float32)
    ).astype(jnp.bfloat16)
    features = HEADS * HEAD
    value_part = jnp.einsum("hqk,qhd->khd", weights, cotangent, preferred_element_type=jnp.float32)
    key_part = softmax_scale * jnp.einsum(
        "hqk,qhd->khd", score_grads, query_heads, preferred_element_type=jnp.float32
    )
    summed = lax.psum_scatter(
        jnp.concatenate(
            [
                key_part.reshape(lax.axis_size("ctx") * local_rows, features),
                value_part.reshape(lax.axis_size("ctx") * local_rows, features),
            ],
            axis=1,
        ),
        "ctx",
        scatter_dimension=0,
        tiled=True,
    )
    key_grads = summed[:, :features].astype(jnp.bfloat16)
    value_grads = summed[:, features:].astype(jnp.bfloat16)
    return (
        attended.reshape(local_rows, features),
        query_grads.reshape(local_rows, features),
        key_grads,
        value_grads,
    )


def solution(mesh):
    return jax.shard_map(
        on_device,
        mesh=mesh,
        in_specs=(
            P(("dp", "ctx"), None),
            P(("dp", "ctx"), None),
            P(("dp", "ctx"), None),
            P(("dp", "ctx"), None),
        ),
        out_specs=(
            P(("dp", "ctx"), None),
            P(("dp", "ctx"), None),
            P(("dp", "ctx"), None),
            P(("dp", "ctx"), None),
        ),
        check_vma=False,
    )
```

profile of v0, /device:TPU:0, one launch (start us, length us, event | category | flops | bytes accessed | tf_op | source)
XLA Modules:
  0.0 541.9 jit_solution(15836388392980093392)
XLA Ops:
  7.2 0.0 all-gather.3.cloned.1.call-start
  7.2 2.0 copy.19
  9.3 0.0 all-gather.3.cloned.1.call-update
  9.3 0.0 all-gather.5.cloned.1.call-start
  9.3 0.7 all-gather.5.cloned.1.call-update
  10.0 0.0 reduce-scatter.2.cloned.1.call-start
  10.1 1.2 copy.23
  11.3 1.2 copy.34
  12.6 78.0 %all-gather.3.cloned.1.call-done = bf16[4096,1024]{0,1:T(8,128)(2,1)} async-done(((bf16[256,1024]{0,1:T(8,128)(2,1)}), bf16[4096,1024]{0,1:T(8,128)(2,1)}) %all-gather.3.cloned.1.call-update) | async-done | bytes 8388624 | tf_op jit(solution)/shard_map/all_gather | solution.py:16
  90.6 17.1 %multiply_reduce_fusion = (f32[8,256]{1,0:T(8,128)S(1)}, f32[8,256,4096]{2,1,0:T(8,128)}) fusion(bf16[256,8,128]{0,2,1:T(8,128)(2,1)S(1)} %bitcast.37, bf16[4096,8,128]{0,2,1:T(8,128)(2,1)} %bitcast.35), kind=kOutput, calls=%fused_computation.4 | convolution fusion | flops 2164258816 | bytes 42475520 | tf_op jit(solution)/shard_map/qhd,khd->hqk/dot_general | solution.py:23
  107.7 0.0 copy-start
  107.7 15.3 %exponential_reduce_fusion = f32[8,256]{1,0:T(8,128)S(1)} fusion(f32[8,256,4096]{2,1,0:T(8,128)} %get-tuple-element.15, f32[8,256]{1,0:T(8,128)S(1)} %get-tuple-element.14), kind=kLoop, calls=%fused_computation.3 | loop fusion | flops 25163776 | bytes 33570816 | tf_op jit(solution)/shard_map/reduce_sum | solution.py:27
  123.0 6.1 %copy-done = f32[8,256,4096]{2,1,0:T(8,128)S(1)} copy-done((f32[8,256,4096]{2,1,0:T(8,128)S(1)}, f32[8,256,4096]{2,1,0:T(8,128)}, u32[]{:S(2)}) %copy-start) | copy-done | bytes 33554456
  129.1 8.9 %exponential_convert_fusion = bf16[8,256,4096]{2,1,0:T(8,128)(2,1)} fusion(f32[8,256,4096]{2,1,0:T(8,128)S(1)} %copy-done, f32[8,256]{1,0:T(8,128)S(1)} %log_add_fusion), kind=kLoop, calls=%fused_computation.2 | loop fusion | flops 25165824 | bytes 50339840 | tf_op jit(solution)/shard_map/convert_element_type | solution.py:28
  138.0 25.6 %all-gather.5.cloned.1.call-done = bf16[4096,1024]{1,0:T(8,128)(2,1)} async-done(((bf16[256,1024]{1,0:T(8,128)(2,1)}), bf16[4096,1024]{1,0:T(8,128)(2,1)}) %all-gather.5.cloned.1.call-update) | async-done | bytes 8388624 | tf_op jit(solution)/shard_map/all_gather | solution.py:17
  163.7 12.0 %copy.22 = bf16[4096,1024]{0,1:T(8,128)(2,1)} copy(bf16[4096,1024]{1,0:T(8,128)(2,1)} %all-gather.5.cloned.1.call-done) | data formatting | bytes 16777216 | tf_op jit(solution)/shard_map/all_gather | solution.py:17
  175.7 11.2 %multiply_reduce_fusion.1 = (f32[256,8]{0,1:T(8,128)S(1)}, bf16[8,256,128]{1,2,0:T(8,128)(2,1)S(1)}) fusion(bf16[256,1024]{0,1:T(8,128)(2,1)S(1)} %copy.23, bf16[8,256,4096]{2,1,0:T(8,128)(2,1)} %exponential_convert_fusion, bf16[4096,8,128]{0,2,1:T(8,128)(2,1)} %bitcast.33), kind=kOutput, calls=%fused_computation.9 | convolution fusion | flops 2148792320 | bytes 26222592 | tf_op jit(solution)/shard_map/hqk,khd->qhd/dot_general | solution.py:29
  186.9 13.9 %fusion.2 = f32[8,4096,128]{1,2,0:T(8,128)} fusion(bf16[256,8,128]{0,2,1:T(8,128)(2,1)S(1)} %bitcast.39, bf16[8,256,4096]{2,1,0:T(8,128)(2,1)} %exponential_convert_fusion), kind=kOutput, calls=%fused_computation.12 | convolution fusion | flops 2147483648 | bytes 34078720 | tf_op jit(solution)/shard_map/hqk,qhd->khd/dot_general | solution.py:44
  200.8 14.3 %multiply_convert_fusion = bf16[8,256,4096]{2,1,0:T(8,128)(2,1)} fusion(bf16[8,256,4096]{2,1,0:T(8,128)(2,1)} %exponential_convert_fusion, f32[8,256]{1,0:T(8,128)S(1)} %bitcast.43, bf16[256,8,128]{0,2,1:T(8,128)(2,1)S(1)} %bitcast.40, bf16[4096,8,128]{0,2,1:T(8,128)(2,1)} %bitcast.34), kind=kOutput, calls=%fused_computation.1 | convolution fusion | flops 2181038080 | bytes 42475520 | tf_op jit(solution)/shard_map/qhd,khd->hqk/dot_general | solution.py:33
  215.1 17.5 %copy.28 = f32[4096,1024]{1,0:T(8,128)} copy(f32[4096,1024]{0,1:T(8,128)} %bitcast.31) | data formatting | bytes 33554432 | tf_op jit(solution)/shard_map/reshape | solution.py:52
  232.6 14.7 %broadcast_multiply_fusion = f32[8,4096,128]{1,2,0:T(8,128)} fusion(bf16[256,8,128]{0,2,1:T(8,128)(2,1)S(1)} %bitcast.38, bf16[8,256,4096]{2,1,0:T(8,128)(2,1)} %multiply_convert_fusion), kind=kOutput, calls=%fused_computation.5 | convolution fusion | flops 2151677952 | bytes 34078720 | tf_op jit(solution)/shard_map/hqk,qhd->khd/dot_general | solution.py:45
  247.2 17.4 %copy.27 = f32[4096,1024]{1,0:T(8,128)} copy(f32[4096,1024]{0,1:T(8,128)} %bitcast.32) | data formatting | bytes 33554432 | tf_op jit(solution)/shard_map/reshape | solution.py:51
  264.7 23.1 %pad_maximum_fusion = f32[4096,2048]{1,0:T(8,128)} fusion(f32[4096,1024]{1,0:T(8,128)} %copy.28, f32[4096,1024]{1,0:T(8,128)} %copy.27), kind=kLoop, calls=%fused_computation | loop fusion | flops 8388608 | bytes 67108864 | tf_op jit(solution)/shard_map/concatenate | solution.py:49
  287.8 0.0 reduce-scatter.2.cloned.1.call-update
  287.8 1.0 copy.29
  288.8 13.0 %fusion = bf16[8,256,128]{1,2,0:T(8,128)(2,1)S(1)} fusion(bf16[8,256,4096]{2,1,0:T(8,128)(2,1)} %multiply_convert_fusion, bf16[4096,8,128]{0,2,1:T(8,128)(2,1)} %bitcast.36), kind=kOutput, calls=%fused_computation.7 | convolution fusion | flops 2148007936 | bytes 25690112 | tf_op jit(solution)/shard_map/hqk,khd->qhd/dot_general | solution.py:41
  301.8 1.0 copy.30
  302.8 229.8 %reduce-scatter.2.cloned.1.call-done = f32[256,2048]{1,0:T(8,128)} async-done(((f32[4096,2048]{1,0:T(8,128)}), f32[256,2048]{1,0:T(8,128)}) %reduce-scatter.2.cloned.1.call-update) | async-done | bytes 2097168 | tf_op jit(solution)/shard_map/reduce_scatter | solution.py:48
  532.6 1.7 convert.4
  534.4 1.0 fusion.1
  (1 shorter events, 0.0 us)
Async XLA Ops:
  7.2 83.4 %all-gather.3.cloned.1.call-start = ((), (), s32[]{:S(2)}) async-start(), calls=%async_computation.1 | async-start | bytes 8912896 | tf_op jit(solution)/shard_map/all_gather | solution.py:16
  9.3 154.4 %all-gather.5.cloned.1.call-start = ((), (), s32[]{:S(2)}) async-start(), calls=%async_computation.2 | async-start | bytes 8912896 | tf_op jit(solution)/shard_map/all_gather | solution.py:17
  10.0 522.6 %reduce-scatter.2.cloned.1.call-start = ((), (), s32[]{:S(2)}) async-start(), calls=%async_computation.3 | async-start | bytes 35651584 | tf_op jit(solution)/shard_map/reduce_scatter | solution.py:48
  107.7 21.4 %copy-start = (f32[8,256,4096]{2,1,0:T(8,128)S(1)}, f32[8,256,4096]{2,1,0:T(8,128)}, u32[]{:S(2)}) copy-start(f32[8,256,4096]{2,1,0:T(8,128)} %get-tuple-element.15) | copy-start | bytes 100663296
Sparse Core Ops, SparseCore 0:
  10.8 79.6 all-gather.2
  93.1 70.5 all-gather.4
  287.9 244.6 reduce-scatter.1
where the time goes:
time: 543 us; the launch traced here: 542 us
  waiting for transfers between devices  334 us (62%)
  matrix products  84.2 us (16%)
  local copies, waits for them, and re-layouts  60.5 us (11%)
  other arithmetic  49.1 us (9%)
  between operations  13.8 us (3%)
    reduce_scatter x1, waiting for transfers between devices, on_device(): lax.psum_scatter(jnp.concatenate([key_part.reshape(lax.axis_size('ctx') *...  230 us
    all_gather x1, waiting for transfers between devices, on_device(): lax.all_gather(keys, 'ctx', axis=0, tiled=True)  78 us
    all_gather x1, waiting for transfers between devices, on_device(): lax.all_gather(values, 'ctx', axis=0, tiled=True)  25.6 us
    concatenate x1, other arithmetic, on_device(): jnp.concatenate([key_part.reshape(lax.axis_size('ctx') * local_rows, feat...  23.1 us
    reshape x1, local copies, waits for them, and re-layouts, on_device(): value_part.reshape(lax.axis_size('ctx') * local_rows, features)  17.5 us
    reshape x1, local copies, waits for them, and re-layouts, on_device(): key_part.reshape(lax.axis_size('ctx') * local_rows, features)  17.4 us
    dot_general x1, matrix products, on_device(): jnp.einsum('qhd,khd->hqk', query_heads, key_heads, preferred_element_type...  17.1 us
    reduce_sum x1, other arithmetic, on_device(): jnp.sum(jnp.exp(scores - row_max), axis=2, keepdims=True)  15.3 us
  transfers between devices with their start and end apart: 3, of which 3 were waited for; matrix products, arithmetic and copies ran while one was open for 11% of the time, Pallas kernels for 0%

commit v1 on v0

v1 whole, which is shorter than its diff:
```python
import functools

import jax
import jax.numpy as jnp
from jax import lax
from jax.experimental import pallas as pl
from jax.experimental.pallas import tpu as pltpu
from jax.sharding import PartitionSpec as P

HEAD = 128
HEADS = 8
SCALE = HEAD**-0.5
LOG2E = 1.4426950408889634
F32 = jnp.float32
BF16 = jnp.bfloat16
NN = (((1,), (0,)), ((), ()))
NT = (((1,), (1,)), ((), ()))
VMEM_LIMIT = 60 * 2**20


def dot(a, b, dims):
    return lax.dot_general(a, b, dims, preferred_element_type=F32)


def rows(i, size):
    return pl.ds(pl.multiple_of(i * size, size), size)


def attention_kernel(
    key_block,
    qd_ref,
    kv_ref,
    kv_far_ref,
    oq_ref,
    near_ref,
    far_ref,
    kk_ref,
    va_ref,
    kt_ref,
    vt_ref,
    q2_ref,
    da_ref,
    s_ref,
    e_ref,
    dk_ref,
    dv_ref,
):
    queries = qd_ref.shape[0]
    half = kv_ref.shape[0]
    keys = 2 * half
    query_block = s_ref.shape[1]
    chunks = keys // key_block
    half_chunks = half // key_block

    def prepare(source, base):
        def step(i, _):
            k = source[rows(i, key_block), 0:HEAD]
            v = source[rows(i, key_block), HEAD : 2 * HEAD]
            to = rows(i + base, key_block)
            kk_ref[to, 0:HEAD] = k
            kk_ref[to, HEAD : 2 * HEAD] = k
            va_ref[to, 0:HEAD] = v
            lane = lax.broadcasted_iota(jnp.int32, (key_block, HEAD), 1)
            va_ref[to, HEAD : 2 * HEAD] = jnp.where(lane < 2, 1.0, 0.0).astype(BF16)
            kt_ref[:, to] = k.T
            vt_ref[0:HEAD, to] = v.T
            vt_ref[HEAD : HEAD + 16, to] = jnp.ones((16, key_block), BF16)
            return 0

        lax.fori_loop(0, half_chunks, step, 0)

    prepare(kv_ref, 0)
    prepare(kv_far_ref, half_chunks)

    def block(b, _):
        at = rows(b, query_block)
        q = qd_ref[at, 0:HEAD]
        grad = qd_ref[at, HEAD : 2 * HEAD]
        scaled = q.astype(F32) * (SCALE * LOG2E)
        high = scaled.astype(BF16)
        q2_ref[:, 0:HEAD] = high
        q2_ref[:, HEAD : 2 * HEAD] = (scaled - high.astype(F32)).astype(BF16)

        def scores(i, top):
            r = rows(i, key_block)
            s = dot(kk_ref[r, :], q2_ref[...], NT)
            s_ref[r, :] = s
            return jnp.maximum(top, jnp.max(s.reshape(key_block // 8, 8, query_block), axis=0))

        top = lax.fori_loop(0, chunks, scores, jnp.full((8, query_block), -jnp.inf, F32))
        top = jnp.max(top, axis=0, keepdims=True)

        def weigh(i, total):
            r = rows(i, key_block)
            e = jnp.exp2(s_ref[r, :] - top).astype(BF16)
            e_ref[r, :] = e
            return total + dot(vt_ref[:, r], e, NN)

        total = lax.fori_loop(0, chunks, weigh, jnp.zeros((HEAD + 16, query_block), F32))
        inverse = 1.0 / total[HEAD : HEAD + 1, :]
        attended = (total[0:HEAD, :] * inverse).T.astype(BF16)
        oq_ref[at, 0:HEAD] = attended
        row_dots = jnp.sum(
            grad.astype(F32) * attended.astype(F32), axis=1, keepdims=True
        )
        dots_high = row_dots.astype(BF16).astype(F32)
        lane = lax.broadcasted_iota(jnp.int32, (query_block, HEAD), 1)
        da_ref[:, 0:HEAD] = grad
        da_ref[:, HEAD : 2 * HEAD] = jnp.where(
            lane == 0, -dots_high, jnp.where(lane == 1, dots_high - row_dots, 0.0)
        ).astype(BF16)
        inverse_column = jnp.broadcast_to(inverse, (8, query_block)).T[:, 0:1]
        grad_over = (grad.astype(F32) * inverse_column).astype(BF16)
        query_over = (q.astype(F32) * (inverse_column * SCALE)).astype(BF16)

        def back(i, total):
            r = rows(i, key_block)
            e = e_ref[r, :]
            g = (e.astype(F32) * dot(va_ref[r, :], da_ref[...], NT)).astype(BF16)
            dv = dot(e, grad_over, NN)
            dk = dot(g, query_over, NN)

            @pl.when(b == 0)
            def _():
                dv_ref[r, :] = dv
                dk_ref[r, :] = dk

            @pl.when(b > 0)
            def _():
                dv_ref[r, :] += dv
                dk_ref[r, :] += dk

            return total + dot(kt_ref[:, r], g, NN)

        total = lax.fori_loop(0, chunks, back, jnp.zeros((HEAD, query_block), F32))
        oq_ref[at, HEAD : 2 * HEAD] = (total * (inverse * SCALE)).T.astype(BF16)
        return 0

    lax.fori_loop(0, queries // query_block, block, 0)
    near_ref[:, 0:HEAD] = dk_ref[0:half, :]
    near_ref[:, HEAD : 2 * HEAD] = dv_ref[0:half, :]
    far_ref[:, 0:HEAD] = dk_ref[half:keys, :].astype(BF16)
    far_ref[:, HEAD : 2 * HEAD] = dv_ref[half:keys, :].astype(BF16)


def attention(qd, kv, kv_far, key_block=1024, query_block=1024):
    queries, half = qd.shape[0], kv.shape[0]
    keys = 2 * half
    return pl.pallas_call(
        functools.partial(attention_kernel, key_block),
        out_shape=(
            jax.ShapeDtypeStruct((queries, 2 * HEAD), BF16),
            jax.ShapeDtypeStruct((half, 2 * HEAD), F32),
            jax.ShapeDtypeStruct((half, 2 * HEAD), BF16),
        ),
        scratch_shapes=[
            pltpu.VMEM((keys, 2 * HEAD), BF16),
            pltpu.VMEM((keys, 2 * HEAD), BF16),
            pltpu.VMEM((HEAD, keys), BF16),
            pltpu.VMEM((HEAD + 16, keys), BF16),
            pltpu.VMEM((query_block, 2 * HEAD), BF16),
            pltpu.VMEM((query_block, 2 * HEAD), BF16),
            pltpu.VMEM((keys, query_block), F32),
            pltpu.VMEM((keys, query_block), BF16),
            pltpu.VMEM((keys, HEAD), F32),
            pltpu.VMEM((keys, HEAD), F32),
        ],
        compiler_params=pltpu.CompilerParams(vmem_limit_bytes=VMEM_LIMIT),
        cost_estimate=pl.CostEstimate(
            flops=12 * queries * keys * HEAD,
            bytes_accessed=12 * queries * HEAD,
            transcendentals=queries * keys,
        ),
        name="attention",
    )(qd, kv, kv_far)


def pack_kernel(q_ref, k_ref, v_ref, g_ref, out_ref):
    out_ref[0, 0, :, 0:HEAD] = q_ref[...]
    out_ref[0, 0, :, HEAD : 2 * HEAD] = g_ref[...]
    out_ref[0, 1, :, 0:HEAD] = k_ref[...]
    out_ref[0, 1, :, HEAD : 2 * HEAD] = v_ref[...]


def pack(queries, keys, values, grad_out):
    tokens = queries.shape[0]
    spec = pl.BlockSpec((tokens, HEAD), lambda h: (0, h))
    return pl.pallas_call(
        pack_kernel,
        grid=(HEADS,),
        in_specs=[spec] * 4,
        out_specs=pl.BlockSpec((1, 2, tokens, 2 * HEAD), lambda h: (h, 0, 0, 0)),
        out_shape=jax.ShapeDtypeStruct((HEADS, 2, tokens, 2 * HEAD), BF16),
        name="pack",
    )(queries, keys, values, grad_out)


def join_kernel(oq_ref, near_ref, far_ref, out_ref):
    out_ref[0, 0] = oq_ref[...]
    out_ref[0, 1] = (near_ref[...] + far_ref[...].astype(F32)).astype(BF16)


def join(oq, near, far):
    tokens = oq.shape[0] // HEADS
    spec = pl.BlockSpec((tokens, 2 * HEAD), lambda h: (h, 0))
    return pl.pallas_call(
        join_kernel,
        grid=(HEADS,),
        in_specs=[spec] * 3,
        out_specs=pl.BlockSpec((1, 2, tokens, 2 * HEAD), lambda h: (h, 0, 0, 0)),
        out_shape=jax.ShapeDtypeStruct((HEADS, 2, tokens, 2 * HEAD), BF16),
        name="join",
    )(oq, near, far)


def unpack_kernel(in_ref, o_ref, dq_ref, dk_ref, dv_ref):
    o_ref[...] = in_ref[0, 0, :, 0:HEAD]
    dq_ref[...] = in_ref[0, 0, :, HEAD : 2 * HEAD]
    dk_ref[...] = in_ref[0, 1, :, 0:HEAD]
    dv_ref[...] = in_ref[0, 1, :, HEAD : 2 * HEAD]


def unpack(packed):
    tokens = packed.shape[2]
    spec = pl.BlockSpec((tokens, HEAD), lambda h: (0, h))
    return pl.pallas_call(
        unpack_kernel,
        grid=(HEADS,),
        in_specs=[pl.BlockSpec((1, 2, tokens, 2 * HEAD), lambda h: (h, 0, 0, 0))],
        out_specs=[spec] * 4,
        out_shape=[jax.ShapeDtypeStruct((tokens, HEADS * HEAD), BF16)] * 4,
        name="unpack",
    )(packed)


def on_device(queries, keys, values, grad_out):
    members = lax.axis_size("ctx")
    same_core = [list(range(core, members, 2)) for core in range(2)]
    other_core = [(i, i ^ 1) for i in range(members)]
    swap = functools.partial(
        lax.all_to_all,
        axis_name="ctx",
        split_axis=0,
        concat_axis=0,
        tiled=True,
        axis_index_groups=same_core,
    )
    got = swap(pack(queries, keys, values, grad_out))
    tokens = queries.shape[0]
    qd = got[:, 0].reshape(HEADS * tokens, 2 * HEAD)
    kv = got[:, 1].reshape(HEADS * tokens, 2 * HEAD)
    kv_far = lax.ppermute(kv, "ctx", other_core)
    oq, near, far = attention(qd, kv, kv_far)
    far = lax.ppermute(far, "ctx", other_core)
    return tuple(unpack(swap(join(oq, near, far))))


def solution(mesh):
    spec = P(("dp", "ctx"), None)
    return jax.shard_map(
        on_device,
        mesh=mesh,
        in_specs=(spec,) * 4,
        out_specs=(spec,) * 4,
        check_vma=False,
    )
```

time: 543 us -> 137 us (0.25)
  waiting for transfers between devices: 334 us -> 5.39 us
  matrix products: 84.2 us -> 0 us
  blocking collectives: 0 us -> 69.4 us
  local copies, waits for them, and re-layouts: 60.5 us -> 3.16 us
  Pallas kernels: 0 us -> 57.3 us
  other arithmetic: 49.1 us -> 0 us
  between operations: 13.8 us -> 0.64 us
    reduce_scatter x1 -> x0, waiting for transfers between devices: 230 us -> none  [on_device(): lax.psum_scatter(jnp.concatenate([key_part.reshape(lax.axis_size('ctx') *...]
    all_gather x2 -> x0, waiting for transfers between devices: 104 us -> none  [the longest x1 78 us: on_device(): lax.all_gather(keys, 'ctx', axis=0, tiled=True)]
    dot_general x6 -> x0, matrix products: 84.2 us -> none  [the longest x1 17.1 us: on_device(): jnp.einsum('qhd,khd->hqk', query_heads, key_heads, preferred_element_type...]
    all_to_all x0 -> x2, blocking collectives: none -> 69.4 us  [the longest x1 36.2 us: on_device(): got = swap(pack(queries, keys, values, grad_out))]
    pallas_call x0 -> x4, Pallas kernels: none -> 57.3 us  [the longest x1 39.7 us: attention(): pl.pallas_call(functools.partial(attention_kernel, key_block), out_shape=...]
    reshape x3 -> x0, local copies, waits for them, and re-layouts: 36.1 us -> none  [the longest x1 17.5 us: on_device(): value_part.reshape(lax.axis_size('ctx') * local_rows, features)]
    concatenate x1 -> x0, other arithmetic: 23.1 us -> none  [on_device(): jnp.concatenate([key_part.reshape(lax.axis_size('ctx') * local_rows, feat...]
    reduce_sum x1 -> x0, other arithmetic: 15.3 us -> none  [on_device(): jnp.sum(jnp.exp(scores - row_max), axis=2, keepdims=True)]
  transfers between devices with their start and end apart: 3 -> 2, of which waited for: 3 -> 2; matrix products, arithmetic and copies ran while one was open for 11% -> 0% of each run, Pallas kernels for 0% -> 0%
where the time goes in v1:
time: 137 us; the launch traced here: 136 us
  blocking collectives  69.4 us (51%)
  Pallas kernels  57.3 us (42%)
  waiting for transfers between devices  5.39 us (4%)
  local copies, waits for them, and re-layouts  3.16 us (2%)
    pallas_call x1, Pallas kernels, attention(): pl.pallas_call(functools.partial(attention_kernel, key_block), out_shape=...  39.7 us
    all_to_all x1, blocking collectives, on_device(): got = swap(pack(queries, keys, values, grad_out))  36.2 us
    all_to_all x1, blocking collectives, on_device(): return tuple(unpack(swap(join(oq, near, far))))  33.2 us
    pallas_call x1, Pallas kernels, join(): pl.pallas_call(join_kernel, grid=(HEADS,), in_specs=[spec] * 3, out_specs...  6.05 us
    pallas_call x1, Pallas kernels, pack(): pl.pallas_call(pack_kernel, grid=(HEADS,), in_specs=[spec] * 4, out_specs...  5.76 us
    pallas_call x1, Pallas kernels, unpack(): pl.pallas_call(unpack_kernel, grid=(HEADS,), in_specs=[pl.BlockSpec((1, 2...  5.73 us
  transfers between devices with their start and end apart: 2, of which 2 were waited for; matrix products, arithmetic and copies ran while one was open for 0% of the time, Pallas kernels for 0%

profile of v1, /device:TPU:0, one launch (start us, length us, event | category | flops | bytes accessed | tf_op | source)
XLA Modules:
  0.0 136.0 jit_solution(12290997268479907515)
XLA Ops:
  0.6 5.8 %pack.1 = bf16[8,2,256,256]{3,2,1,0:T(8,128)(2,1)} custom-call(bf16[256,1024]{1,0:T(8,128)(2,1)} %q_ref.1, bf16[256,1024]{1,0:T(8,128)(2,1)} %k_ref.1, bf16[256,1024]{1,0:T(8,128)(2,1)} %v_ref.1, bf16[256,1024]{1,0:T(8,128)(2,1)} %g_ref.1), custom_call_target="tpu_custom_call" | custom-call | tf_op jit(solution)/shard_map/pack/pallas_call | solution.py:188
  6.4 36.2 %all_to_all.10 = bf16[8,2,256,256]{3,2,1,0:T(8,128)(2,1)S(1)} all-to-all(bf16[8,2,256,256]{3,2,1,0:T(8,128)(2,1)} %pack.1), channel_id=1, replica_groups={{0,2,4,6,8,10,12,14},{1,3,5,7,9,11,13,15},{16,18,20,22,24,26,28,30},{17..., dimensions={0} | all-to-all | bytes 4194304 | tf_op jit(solution)/shard_map/all_to_all | solution.py:248
  42.6 1.2 fusion
  43.8 0.0 copy-start
  43.8 0.0 collective-permute-start
  43.8 2.7 %collective-permute-done.kv_far_ref = bf16[2048,256]{1,0:T(8,128)(2,1)S(1)} collective-permute-done((bf16[2048,256]{1,0:T(8,128)(2,1)S(1)}, bf16[2048,256]{1,0:T(8,128)(2,1)S(1)}, u32[]{:S(2)}, u32[]{:S(2)}) %collective-permute-start) | collective-permute-done | bytes 1048608 | tf_op jit(solution)/shard_map/ppermute | solution.py:252
  46.4 0.0 copy-start.2
  46.4 0.0 copy-done
  46.5 1.0 copy-done.2
  47.4 39.7 %attention.1 = (bf16[2048,256]{1,0:T(8,128)(2,1)}, f32[2048,256]{1,0:T(8,128)}, bf16[2048,256]{1,0:T(8,128)(2,1)}) custom-call(bf16[2048,256]{1,0:T(8,128)(2,1)} %bitcast.4, bf16[2048,256]{1,0:T(8,128)(2,1)} %bitcast.3, bf16[2048,256]{1,0:T(8,128)(2,1)} %copy-done.2), custom_call_target="tpu_custom_call" | custom-call | flops 12884901888 | bytes 3145728 | tf_op jit(solution)/shard_map/attention/pallas_call | solution.py:149
  87.2 0.1 collective-permute-start.1
  87.3 2.7 %collective-permute-done.1.far_ref = bf16[2048,256]{1,0:T(8,128)(2,1)S(1)} collective-permute-done((bf16[2048,256]{1,0:T(8,128)(2,1)}, bf16[2048,256]{1,0:T(8,128)(2,1)S(1)}, u32[]{:S(2)}, u32[]{:S(2)}) %collective-permute-start.1) | collective-permute-done | bytes 1048608 | tf_op jit(solution)/shard_map/ppermute | solution.py:254
  90.0 0.0 copy-start.1
  90.0 1.0 copy-done.1
  91.0 6.0 %join.1 = bf16[8,2,256,256]{3,2,1,0:T(8,128)(2,1)} custom-call(bf16[2048,256]{1,0:T(8,128)(2,1)} %get-tuple-element.7.oq_ref, f32[2048,256]{1,0:T(8,128)} %get-tuple-element.8.near_ref, bf16[2048,256]{1,0:T(8,128)(2,1)} %copy-done.1), custom_call_target="tpu_custom_call" | custom-call | tf_op jit(solution)/shard_map/join/pallas_call | solution.py:206
  97.1 33.2 %all_to_all.11.in_ref = bf16[8,2,256,256]{3,2,1,0:T(8,128)(2,1)} all-to-all(bf16[8,2,256,256]{3,2,1,0:T(8,128)(2,1)} %join.1), channel_id=1, replica_groups={{0,2,4,6,8,10,12,14},{1,3,5,7,9,11,13,15},{16,18,20,22,24,26,28,30},{17..., dimensions={0} | all-to-all | bytes 4194304 | tf_op jit(solution)/shard_map/all_to_all | solution.py:255
  130.3 5.7 %unpack.1 = (bf16[256,1024]{1,0:T(8,128)(2,1)}, bf16[256,1024]{1,0:T(8,128)(2,1)}, bf16[256,1024]{1,0:T(8,128)(2,1)}, bf16[256,1024]{1,0:T(8,128)(2,1)}) custom-call(bf16[8,2,256,256]{3,2,1,0:T(8,128)(2,1)} %all_to_all.11.in_ref), custom_call_target="tpu_custom_call" | custom-call | tf_op jit(solution)/shard_map/unpack/pallas_call | solution.py:226
Async XLA Ops:
  43.8 2.7 %copy-start = (bf16[8,1,256,256]{3,2,1,0:T(8,128)(2,1)}, bf16[8,1,256,256]{3,2,1,0:T(8,128)(2,1)S(1)}, u32[]{:S(2)}) copy-start(bf16[8,1,256,256]{3,2,1,0:T(8,128)(2,1)S(1)} %get-tuple-element.10) | copy-start | bytes 3145732
  43.8 2.7 %collective-permute-start = (bf16[2048,256]{1,0:T(8,128)(2,1)S(1)}, bf16[2048,256]{1,0:T(8,128)(2,1)S(1)}, u32[]{:S(2)}, u32[]{:S(2)}) collective-permute-start(bf16[2048,256]{1,0:T(8,128)(2,1)S(1)} %bitcast.2), channel_id=1, source_target_pairs={{0,1},{1,0},{2,3},{3,2},{4,5},{5,4},{6,7},{7,6},{8,9},{9,8},{10,11... | collective-permute-start | bytes 3145736 | tf_op jit(solution)/shard_map/ppermute | solution.py:252
  46.4 1.0 copy-start.2
  87.2 2.9 %collective-permute-start.1 = (bf16[2048,256]{1,0:T(8,128)(2,1)}, bf16[2048,256]{1,0:T(8,128)(2,1)S(1)}, u32[]{:S(2)}, u32[]{:S(2)}) collective-permute-start(bf16[2048,256]{1,0:T(8,128)(2,1)} %get-tuple-element.9), channel_id=1, source_target_pairs={{0,1},{1,0},{2,3},{3,2},{4,5},{5,4},{6,7},{7,6},{8,9},{9,8},{10,11... | collective-permute-start | bytes 3145736 | tf_op jit(solution)/shard_map/ppermute | solution.py:254
  90.0 1.0 copy-start.1

commit v2 on v0

v2 whole, which is shorter than its diff:
```python
import functools

import jax
import jax.numpy as jnp
from jax import lax
from jax.experimental import pallas as pl
from jax.experimental.pallas import tpu as pltpu
from jax.sharding import PartitionSpec as P

HEAD = 128
HEADS = 8
SCALE = HEAD**-0.5
LOG2E = 1.4426950408889634
F32 = jnp.float32
BF16 = jnp.bfloat16
NN = (((1,), (0,)), ((), ()))
NT = (((1,), (1,)), ((), ()))
VMEM_LIMIT = 60 * 2**20


def dot(a, b, dims):
    return lax.dot_general(a, b, dims, preferred_element_type=F32)


def rows(i, size):
    return pl.ds(pl.multiple_of(i * size, size), size)


def lanes(shape):
    return lax.broadcasted_iota(jnp.int32, shape, 1)


def attend_kernel(
    key_block,
    got_ref,
    far_ref,
    out_ref,
    dv_far_ref,
    grad_ref,
    query_ref,
    inverse_ref,
    weights_hbm,
    kk_ref,
    vt_ref,
    q2_ref,
    m_ref,
    total_ref,
    e_ref,
    over_ref,
    sem,
):
    blocks, _, tokens, _ = got_ref.shape
    half = blocks * tokens
    keys = 2 * half
    queries = half
    chunks = keys // key_block
    half_chunks = chunks // 2
    per_chunk = key_block // tokens

    def prepare(load, base, top):
        def step(i, top):
            pair = load(pl.ds(i * per_chunk, per_chunk)).reshape(key_block, 2 * HEAD)
            k = pair[:, 0:HEAD]
            to = rows(i + base, key_block)
            kk_ref[to, 0:HEAD] = k
            kk_ref[to, HEAD : 2 * HEAD] = k
            vt_ref[0:HEAD, to] = pair[:, HEAD : 2 * HEAD].T
            vt_ref[HEAD : HEAD + 16, to] = jnp.ones((16, key_block), BF16)
            return jnp.maximum(top, dot(ones, k * k, NT))

        return lax.fori_loop(0, half_chunks, step, top)

    ones = jnp.ones((8, HEAD), BF16)
    top = jnp.zeros((8, key_block), F32)
    top = prepare(lambda at: got_ref[at, 1], 0, top)
    top = prepare(lambda at: far_ref[at], half_chunks, top)
    top = jnp.max(top, axis=1, keepdims=True)[0:1, :]

    for i in range(blocks):
        to = slice(i * tokens, (i + 1) * tokens)
        q = got_ref[i, 0, :, 0:HEAD]
        scaled = q.astype(F32) * (SCALE * LOG2E)
        high = scaled.astype(BF16)
        q2_ref[to, 0:HEAD] = high
        q2_ref[to, HEAD : 2 * HEAD] = (scaled - high.astype(F32)).astype(BF16)
        size = dot(ones, q * q, NT)[0:1, :]
        m_ref[:, to] = jnp.sqrt(size * top) * (1.01 * SCALE * LOG2E)

    def scores(i):
        return dot(kk_ref[rows(i, key_block), :], q2_ref[...], NT)

    def weigh():
        total_ref[...] = jnp.zeros_like(total_ref)

        def step(i, _):
            r = rows(i, key_block)
            e = jnp.exp2(scores(i) - m_ref[...]).astype(BF16)
            e_ref[r, :] = e
            total_ref[...] += dot(vt_ref[:, r], e, NN)
            return 0

        lax.fori_loop(0, chunks, step, 0)

    weigh()

    @pl.when(jnp.min(total_ref[HEAD : HEAD + 1, :]) < 2.0**-80)
    def _():
        def step(i, top):
            s = scores(i).reshape(key_block // 8, 8, queries)
            return jnp.maximum(top, jnp.max(s, axis=0))

        top = lax.fori_loop(0, chunks, step, jnp.full((8, queries), -jnp.inf, F32))
        m_ref[...] = jnp.max(top, axis=0, keepdims=True)
        weigh()

    inverse = 1.0 / total_ref[HEAD : HEAD + 1, :]
    inverse_ref[...] = jnp.broadcast_to(inverse, inverse_ref.shape)
    for i in range(blocks):
        to = slice(i * tokens, (i + 1) * tokens)
        part = jnp.broadcast_to(inverse[:, to], (HEAD, tokens))
        attended = (total_ref[0:HEAD, to] * part).T.astype(BF16)
        out_ref[to, 0:HEAD] = attended
        column = part.T
        grad = got_ref[i, 0, :, HEAD : 2 * HEAD]
        grad_wide = grad.astype(F32)
        dots = jnp.sum(grad_wide * attended.astype(F32), axis=1, keepdims=True)
        dots_high = dots.astype(BF16).astype(F32)
        lane = lanes((tokens, HEAD))
        grad_ref[to, 0:HEAD] = grad
        grad_ref[to, HEAD : 2 * HEAD] = jnp.where(
            lane == 0, -dots_high, jnp.where(lane == 1, dots_high - dots, 0.0)
        ).astype(BF16)
        over_ref[to, :] = (grad_wide * column).astype(BF16)
        q = got_ref[i, 0, :, 0:HEAD].astype(F32)
        query_ref[to, :] = (q * (column * SCALE)).astype(BF16)

    def send(i):
        r = rows(i, key_block)
        return pltpu.make_async_copy(e_ref.at[r, :], weights_hbm.at[r, :], sem.at[i])

    for i in range(chunks):
        send(i).start()

    def far(i, _):
        r = rows(i + half_chunks, key_block)
        dv_far_ref[rows(i, key_block), :] = dot(e_ref[r, :], over_ref[...], NN).astype(BF16)
        return 0

    def near(i, _):
        r = rows(i, key_block)
        out_ref[r, HEAD : 2 * HEAD] = dot(e_ref[r, :], over_ref[...], NN).astype(BF16)
        return 0

    lax.fori_loop(0, half_chunks, far, 0)
    lax.fori_loop(0, half_chunks, near, 0)
    for i in range(chunks):
        send(i).wait()


def attend(got, far, key_block=1024):
    blocks, _, tokens, _ = got.shape
    half = blocks * tokens
    keys = 2 * half
    vmem = pl.BlockSpec(memory_space=pltpu.VMEM)
    return pl.pallas_call(
        functools.partial(attend_kernel, key_block),
        out_shape=(
            jax.ShapeDtypeStruct((half, 2 * HEAD), BF16),
            jax.ShapeDtypeStruct((half, HEAD), BF16),
            jax.ShapeDtypeStruct((half, 2 * HEAD), BF16),
            jax.ShapeDtypeStruct((half, HEAD), BF16),
            jax.ShapeDtypeStruct((8, half), F32),
            jax.ShapeDtypeStruct((keys, half), BF16),
        ),
        out_specs=(vmem,) * 5 + (pl.BlockSpec(memory_space=pl.ANY),),
        scratch_shapes=[
            pltpu.VMEM((keys, 2 * HEAD), BF16),
            pltpu.VMEM((HEAD + 16, keys), BF16),
            pltpu.VMEM((half, 2 * HEAD), BF16),
            pltpu.VMEM((1, half), F32),
            pltpu.VMEM((HEAD + 16, half), F32),
            pltpu.VMEM((keys, half), BF16),
            pltpu.VMEM((half, HEAD), BF16),
            pltpu.SemaphoreType.DMA((keys // key_block,)),
        ],
        compiler_params=pltpu.CompilerParams(vmem_limit_bytes=VMEM_LIMIT),
        cost_estimate=pl.CostEstimate(
            flops=6 * half * keys * HEAD,
            bytes_accessed=2 * half * keys,
            transcendentals=half * keys,
        ),
        name="attend",
    )(got, far)


def grads_kernel(
    got_ref,
    far_ref,
    grad_ref,
    query_ref,
    inverse_ref,
    e_ref,
    out_ref,
    dk_far_ref,
    kt_ref,
    va_ref,
    total_ref,
):
    i = pl.program_id(0)
    chunks = pl.num_programs(0)
    half_chunks = chunks // 2
    key_block = e_ref.shape[0]
    tokens = got_ref.shape[2]
    per_chunk = key_block // tokens

    @pl.when(i == 0)
    def _():
        total_ref[...] = jnp.zeros_like(total_ref)
        lane = lanes((key_block, HEAD))
        va_ref[:, HEAD : 2 * HEAD] = jnp.where(lane < 2, 1.0, 0.0).astype(BF16)

    def take(pair):
        pair = pair.reshape(key_block, 2 * HEAD)
        kt_ref[...] = pair[:, 0:HEAD].T
        va_ref[:, 0:HEAD] = pair[:, HEAD : 2 * HEAD]

    @pl.when(i < half_chunks)
    def _():
        take(far_ref[pl.ds(i * per_chunk, per_chunk)])

    @pl.when(i >= half_chunks)
    def _():
        take(got_ref[pl.ds((i - half_chunks) * per_chunk, per_chunk), 1])

    g = (e_ref[...].astype(F32) * dot(va_ref[...], grad_ref[...], NT)).astype(BF16)
    dk = dot(g, query_ref[...], NN).astype(BF16)
    total_ref[...] += dot(kt_ref[...], g, NN)

    @pl.when(i < half_chunks)
    def _():
        dk_far_ref[rows(i, key_block), :] = dk

    @pl.when(i >= half_chunks)
    def _():
        out_ref[rows(i - half_chunks, key_block), HEAD : 2 * HEAD] = dk

    @pl.when(i == chunks - 1)
    def _():
        scaled = total_ref[...] * (inverse_ref[0:1, :] * SCALE)
        out_ref[:, 0:HEAD] = scaled.T.astype(BF16)


def grads(got, far, grad, query, inverse, weights, key_block=1024):
    blocks, _, tokens, _ = got.shape
    half = blocks * tokens
    keys = 2 * half
    chunks = keys // key_block
    whole = pl.BlockSpec(memory_space=pltpu.VMEM)
    return pl.pallas_call(
        grads_kernel,
        grid=(chunks,),
        in_specs=[whole] * 5
        + [pl.BlockSpec((key_block, half), lambda i: ((i + chunks // 2) % chunks, 0))],
        out_specs=(whole, whole),
        out_shape=(
            jax.ShapeDtypeStruct((half, 2 * HEAD), BF16),
            jax.ShapeDtypeStruct((half, HEAD), BF16),
        ),
        scratch_shapes=[
            pltpu.VMEM((HEAD, key_block), BF16),
            pltpu.VMEM((key_block, 2 * HEAD), BF16),
            pltpu.VMEM((HEAD, half), F32),
        ],
        compiler_params=pltpu.CompilerParams(vmem_limit_bytes=VMEM_LIMIT),
        cost_estimate=pl.CostEstimate(
            flops=6 * half * keys * HEAD, bytes_accessed=2 * half * keys, transcendentals=0
        ),
        name="grads",
    )(got, far, grad, query, inverse, weights)


ANY = pl.BlockSpec(memory_space=pl.ANY)


def pack_kernel(q_ref, k_ref, v_ref, g_ref, out_ref, buffer, in_sem, out_sem):
    sources = (q_ref, g_ref, k_ref, v_ref)
    loads = [
        pltpu.make_async_copy(ref, buffer.at[i], in_sem.at[i]) for i, ref in enumerate(sources)
    ]
    for load in loads:
        load.start()
    stores = []
    for i, load in enumerate(loads):
        load.wait()
        for h in range(HEADS):
            store = pltpu.make_async_copy(
                buffer.at[i, :, h * HEAD : (h + 1) * HEAD],
                out_ref.at[h, i // 2, :, (i % 2) * HEAD : (i % 2 + 1) * HEAD],
                out_sem.at[i, h],
            )
            store.start()
            stores.append(store)
    for store in stores:
        store.wait()


def pack(queries, keys, values, grad_out):
    tokens = queries.shape[0]
    return pl.pallas_call(
        pack_kernel,
        in_specs=[ANY] * 4,
        out_specs=ANY,
        out_shape=jax.ShapeDtypeStruct((HEADS, 2, tokens, 2 * HEAD), BF16),
        scratch_shapes=[
            pltpu.VMEM((4, tokens, HEADS * HEAD), BF16),
            pltpu.SemaphoreType.DMA((4,)),
            pltpu.SemaphoreType.DMA((4, HEADS)),
        ],
        name="pack",
    )(queries, keys, values, grad_out)


def join_kernel(out_in_ref, far_ref, out_ref, near_buffer, far_buffer, sem):
    del out_in_ref
    part = out_ref.at[:, HEAD : 2 * HEAD]
    loads = (
        pltpu.make_async_copy(part, near_buffer, sem.at[0]),
        pltpu.make_async_copy(far_ref, far_buffer, sem.at[1]),
    )
    for load in loads:
        load.start()
    for load in loads:
        load.wait()
    near_buffer[...] = (near_buffer[...].astype(F32) + far_buffer[...].astype(F32)).astype(BF16)
    store = pltpu.make_async_copy(near_buffer, part, sem.at[2])
    store.start()
    store.wait()


def join(out, far):
    return pl.pallas_call(
        join_kernel,
        in_specs=[ANY] * 2,
        out_specs=ANY,
        out_shape=jax.ShapeDtypeStruct(out.shape, BF16),
        input_output_aliases={0: 0},
        scratch_shapes=[
            pltpu.VMEM(far.shape, BF16),
            pltpu.VMEM(far.shape, BF16),
            pltpu.SemaphoreType.DMA((3,)),
        ],
        name="join",
    )(out, far)


def unpack_kernel(in_ref, first_ref, second_ref, buffer, in_sem, out_sem):
    loads = [
        [
            pltpu.make_async_copy(
                in_ref.at[h, :, i * HEAD : (i + 1) * HEAD],
                buffer.at[i, :, h * HEAD : (h + 1) * HEAD],
                in_sem.at[i, h],
            )
            for h in range(HEADS)
        ]
        for i in range(2)
    ]
    for load in loads[0] + loads[1]:
        load.start()
    stores = []
    for i, ref in enumerate((first_ref, second_ref)):
        for load in loads[i]:
            load.wait()
        store = pltpu.make_async_copy(buffer.at[i], ref, out_sem.at[i])
        store.start()
        stores.append(store)
    for store in stores:
        store.wait()


def unpack(packed):
    tokens = packed.shape[1]
    whole = jax.ShapeDtypeStruct((tokens, HEADS * HEAD), BF16)
    return pl.pallas_call(
        unpack_kernel,
        in_specs=[ANY],
        out_specs=(ANY, ANY),
        out_shape=(whole, whole),
        scratch_shapes=[
            pltpu.VMEM((2, tokens, HEADS * HEAD), BF16),
            pltpu.SemaphoreType.DMA((2, HEADS)),
            pltpu.SemaphoreType.DMA((2,)),
        ],
        name="unpack",
    )(packed)


def on_device(queries, keys, values, grad_out):
    members = lax.axis_size("ctx")
    same_core = [list(range(core, members, 2)) for core in range(2)]
    other_core = [(i, i ^ 1) for i in range(members)]

    def swap(array):
        return lax.all_to_all(
            array, "ctx", 0, 0, tiled=True, axis_index_groups=same_core
        )

    def back(out, far):
        out = join(out, lax.ppermute(far, "ctx", other_core))
        return swap(out.reshape(HEADS, -1, 2 * HEAD))

    got = swap(pack(queries, keys, values, grad_out))
    far = lax.ppermute(got[:, 1], "ctx", other_core)
    first, dv_far, *rest = attend(got, far)
    first = back(first, dv_far)
    second, dk_far = grads(got, far, *rest)
    second = back(second, dk_far)
    attended, value_grads = unpack(first)
    query_grads, key_grads = unpack(second)
    return attended, query_grads, key_grads, value_grads


def solution(mesh):
    spec = P(("dp", "ctx"), None)
    return jax.shard_map(
        on_device,
        mesh=mesh,
        in_specs=(spec,) * 4,
        out_specs=(spec,) * 4,
        check_vma=False,
    )
```

time: 543 us -> 133 us (0.24)
  waiting for transfers between devices: 334 us -> 20.4 us
  matrix products: 84.2 us -> 0 us
  Pallas kernels: 0 us -> 60.9 us
  local copies, waits for them, and re-layouts: 60.5 us -> 2.64 us
  other arithmetic: 49.1 us -> 0 us
  blocking collectives: 0 us -> 36.2 us
  between operations: 13.8 us -> 0.88 us
  starting transfers between devices: 0.12 us -> 11.1 us
    reduce_scatter x1 -> x0, waiting for transfers between devices: 230 us -> none  [on_device(): lax.psum_scatter(jnp.concatenate([key_part.reshape(lax.axis_size('ctx') *...]
    all_gather x2 -> x0, waiting for transfers between devices: 104 us -> none  [the longest x1 78 us: on_device(): lax.all_gather(keys, 'ctx', axis=0, tiled=True)]
    dot_general x6 -> x0, matrix products: 84.2 us -> none  [the longest x1 17.1 us: on_device(): jnp.einsum('qhd,khd->hqk', query_heads, key_heads, preferred_element_type...]
    pallas_call x0 -> x7, Pallas kernels: none -> 60.9 us  [the longest x1 31.8 us: attend(): pl.pallas_call(functools.partial(attend_kernel, key_block), out_shape=(ja...]
    all_to_all x0 -> x1, blocking collectives: none -> 36.2 us  [swap(): lax.all_to_all(array, 'ctx', 0, 0, tiled=True, axis_index_groups=same_core)]
    reshape x3 -> x0, local copies, waits for them, and re-layouts: 36.1 us -> none  [the longest x1 17.5 us: on_device(): value_part.reshape(lax.axis_size('ctx') * local_rows, features)]
    concatenate x1 -> x0, other arithmetic: 23.1 us -> none  [on_device(): jnp.concatenate([key_part.reshape(lax.axis_size('ctx') * local_rows, feat...]
    reduce_sum x1 -> x0, other arithmetic: 15.3 us -> none  [on_device(): jnp.sum(jnp.exp(scores - row_max), axis=2, keepdims=True)]
  transfers between devices with their start and end apart: 3 -> 5, of which waited for: 3 -> 4; matrix products, arithmetic and copies ran while one was open for 11% -> 0% of each run, Pallas kernels for 0% -> 17%
where the time goes in v2:
time: 133 us; the launch traced here: 132 us
  Pallas kernels  60.9 us (46%)
  blocking collectives  36.2 us (27%)
  waiting for transfers between devices  20.4 us (15%)
  starting transfers between devices  11.1 us (8%)
  local copies, waits for them, and re-layouts  2.64 us (2%)
    all_to_all x1, blocking collectives, swap(): lax.all_to_all(array, 'ctx', 0, 0, tiled=True, axis_index_groups=same_core)  36.2 us
    pallas_call x1, Pallas kernels, attend(): pl.pallas_call(functools.partial(attend_kernel, key_block), out_shape=(ja...  31.8 us
    pallas_call x1, Pallas kernels, grads(): pl.pallas_call(grads_kernel, grid=(chunks,), in_specs=[whole] * 5 + [pl.B...  17.6 us
    all_to_all x2, waiting for transfers between devices, swap(): lax.all_to_all(array, 'ctx', 0, 0, tiled=True, axis_index_groups=same_core)  13.7 us
    all_to_all x2, starting transfers between devices, swap(): lax.all_to_all(array, 'ctx', 0, 0, tiled=True, axis_index_groups=same_core)  10.7 us
    pallas_call x2, Pallas kernels, join(): pl.pallas_call(join_kernel, in_specs=[ANY] * 2, out_specs=ANY, out_shape=...  4.38 us
    pallas_call x2, Pallas kernels, unpack(): pl.pallas_call(unpack_kernel, in_specs=[ANY], out_specs=(ANY, ANY), out_s...  4.36 us
    ppermute x2, waiting for transfers between devices, back(): out = join(out, lax.ppermute(far, 'ctx', other_core))  3.97 us
  transfers between devices with their start and end apart: 5, of which 4 were waited for; matrix products, arithmetic and copies ran while one was open for 0% of the time, Pallas kernels for 17%

profile of v2, /device:TPU:0, one launch (start us, length us, event | category | flops | bytes accessed | tf_op | source)
XLA Modules:
  0.0 132.2 jit_solution(12732306390685106207)
XLA Ops:
  0.6 2.7 %pack.1 = bf16[8,2,256,256]{3,2,1,0:T(8,128)(2,1)} custom-call(bf16[256,1024]{1,0:T(8,128)(2,1)} %q_ref.1, bf16[256,1024]{1,0:T(8,128)(2,1)} %k_ref.1, bf16[256,1024]{1,0:T(8,128)(2,1)} %v_ref.1, bf16[256,1024]{1,0:T(8,128)(2,1)} %g_ref.1), custom_call_target="tpu_custom_call" | custom-call | tf_op jit(solution)/shard_map/pack/pallas_call | solution.py:309
  3.4 36.2 %all_to_all.15.got_ref = bf16[8,2,256,256]{3,2,1,0:T(8,128)(2,1)S(1)} all-to-all(bf16[8,2,256,256]{3,2,1,0:T(8,128)(2,1)} %pack.1), channel_id=1, replica_groups={{0,2,4,6,8,10,12,14},{1,3,5,7,9,11,13,15},{16,18,20,22,24,26,28,30},{17..., dimensions={0} | all-to-all | bytes 4194304 | tf_op jit(solution)/shard_map/all_to_all | solution.py:404
  39.6 0.0 copy-start
  39.6 0.1 slice_bitcast_fusion
  39.7 0.1 collective-permute-start
  39.8 2.8 %collective-permute-done.far_ref = bf16[8,256,256]{2,1,0:T(8,128)(2,1)} collective-permute-done((bf16[8,256,256]{2,1,0:T(8,128)(2,1)S(1)}, bf16[8,256,256]{2,1,0:T(8,128)(2,1)}, u32[]{:S(2)}, u32[]{:S(2)}) %collective-permute-start) | collective-permute-done | bytes 1048608 | tf_op jit(solution)/shard_map/ppermute | solution.py:413
  42.6 0.0 copy-done
  42.6 31.8 %attend.1 = (bf16[2048,256]{1,0:T(8,128)(2,1)}, bf16[2048,128]{1,0:T(8,128)(2,1)}, bf16[2048,256]{1,0:T(8,128)(2,1)}, bf16[2048,128]{1,0:T(8,128)(2,1)}, f32[8,2048]{1,0:T(8,128)}, /*index=5*/bf16[4096,2048]{1,0:T(8,128)(2,1)}) custom-call(bf16[8,2,256,256]{3,2,1,0:T(8,128)(2,1)} %copy-done, bf16[8,256,256]{2,1,0:T(8,128)(2,1)} %collective-permute-done.far_ref), custom_call_target="tpu_custom_call" | custom-call | flops 6442450944 | bytes 16777216 | tf_op jit(solution)/shard_map/attend/pallas_call | solution.py:165
  74.4 0.2 collective-permute-start.1
  74.6 2.0 %collective-permute-done.1.far_ref = bf16[2048,128]{1,0:T(8,128)(2,1)S(1)} collective-permute-done((bf16[2048,128]{1,0:T(8,128)(2,1)}, bf16[2048,128]{1,0:T(8,128)(2,1)S(1)}, u32[]{:S(2)}, u32[]{:S(2)}) %collective-permute-start.1) | collective-permute-done | bytes 524320 | tf_op jit(solution)/shard_map/ppermute | solution.py:409
  76.6 0.0 copy-start.4
  76.6 0.8 copy-done.4
  77.4 2.2 %join.2 = bf16[2048,256]{1,0:T(8,128)(2,1)} custom-call(bf16[2048,256]{1,0:T(8,128)(2,1)} %get-tuple-element.16.out_in_ref, bf16[2048,128]{1,0:T(8,128)(2,1)} %copy-done.4), custom_call_target="tpu_custom_call", output_to_operand_aliasing={{}: (0, {})} | custom-call | tf_op jit(solution)/shard_map/join/pallas_call | solution.py:341
  79.6 3.7 %all-to-all-start.1 = ((bf16[8,256,256]{2,1,0:T(8,128)(2,1)}), bf16[8,256,256]{2,1,0:T(8,128)(2,1)S(1)}, u32[]{:S(2)}, u32[]{:S(2)}) async-start(bf16[8,256,256]{2,1,0:T(8,128)(2,1)} %bitcast.7), calls=%async_computation.1 | async-start | bytes 2097152 | tf_op jit(solution)/shard_map/all_to_all | solution.py:404
  83.4 17.6 %grads.1 = (bf16[2048,256]{1,0:T(8,128)(2,1)}, bf16[2048,128]{1,0:T(8,128)(2,1)}) custom-call(bf16[8,2,256,256]{3,2,1,0:T(8,128)(2,1)} %copy-done, bf16[8,256,256]{2,1,0:T(8,128)(2,1)} %collective-permute-done.far_ref, bf16[2048,256]{1,0:T(8,128)(2,1)} %get-tuple-element.19.grad_ref, bf16[2048,128]{1,0:T(8,128)(2,1)} %get-tuple-element.20.query_ref, ...), custom_call_target="tpu_custom_call" | custom-call | flops 6442450944 | bytes 16777216 | tf_op jit(solution)/shard_map/grads/pallas_call | solution.py:259
  100.9 0.1 collective-permute-start.2
  101.1 2.0 %collective-permute-done.2.far_ref = bf16[2048,128]{1,0:T(8,128)(2,1)S(1)} collective-permute-done((bf16[2048,128]{1,0:T(8,128)(2,1)}, bf16[2048,128]{1,0:T(8,128)(2,1)S(1)}, u32[]{:S(2)}, u32[]{:S(2)}) %collective-permute-start.2) | collective-permute-done | bytes 524320 | tf_op jit(solution)/shard_map/ppermute | solution.py:409
  103.1 0.0 copy-start.3
  103.1 0.8 copy-done.3
  103.8 2.2 %join.3 = bf16[2048,256]{1,0:T(8,128)(2,1)} custom-call(bf16[2048,256]{1,0:T(8,128)(2,1)} %get-tuple-element.23.out_in_ref, bf16[2048,128]{1,0:T(8,128)(2,1)} %copy-done.3), custom_call_target="tpu_custom_call", output_to_operand_aliasing={{}: (0, {})} | custom-call | tf_op jit(solution)/shard_map/join/pallas_call | solution.py:341
  106.0 0.0 all-to-all-done.1.in_ref
  106.0 0.0 copy-start.1
  106.1 6.9 %all-to-all-start.2 = ((bf16[8,256,256]{2,1,0:T(8,128)(2,1)}), bf16[8,256,256]{2,1,0:T(8,128)(2,1)S(1)}, u32[]{:S(2)}, u32[]{:S(2)}) async-start(bf16[8,256,256]{2,1,0:T(8,128)(2,1)} %bitcast.6), calls=%async_computation.2 | async-start | bytes 2097152 | tf_op jit(solution)/shard_map/all_to_all | solution.py:404
  113.0 0.0 copy-done.1
  113.0 2.2 %unpack.2 = (bf16[256,1024]{1,0:T(8,128)(2,1)}, bf16[256,1024]{1,0:T(8,128)(2,1)}) custom-call(bf16[8,256,256]{2,1,0:T(8,128)(2,1)} %copy-done.1), custom_call_target="tpu_custom_call" | custom-call | tf_op jit(solution)/shard_map/unpack/pallas_call | solution.py:384
  115.2 13.7 %all-to-all-done.2.in_ref = bf16[8,256,256]{2,1,0:T(8,128)(2,1)S(1)} async-done(((bf16[8,256,256]{2,1,0:T(8,128)(2,1)}), bf16[8,256,256]{2,1,0:T(8,128)(2,1)S(1)}, u32[]{:S(2)}, u32[]{:S(2)}) %all-to-all-start.2) | async-done | bytes 1048608 | tf_op jit(solution)/shard_map/all_to_all | solution.py:404
  128.9 0.0 copy-start.2
  128.9 1.0 copy-done.2
  129.9 2.2 %unpack.3 = (bf16[256,1024]{1,0:T(8,128)(2,1)}, bf16[256,1024]{1,0:T(8,128)(2,1)}) custom-call(bf16[8,256,256]{2,1,0:T(8,128)(2,1)} %copy-done.2), custom_call_target="tpu_custom_call" | custom-call | tf_op jit(solution)/shard_map/unpack/pallas_call | solution.py:384
Async XLA Ops:
  39.6 2.9 %copy-start = (bf16[8,2,256,256]{3,2,1,0:T(8,128)(2,1)}, bf16[8,2,256,256]{3,2,1,0:T(8,128)(2,1)S(1)}, u32[]{:S(2)}) copy-start(bf16[8,2,256,256]{3,2,1,0:T(8,128)(2,1)S(1)} %all_to_all.15.got_ref) | copy-start | bytes 6291460
  39.7 2.9 %collective-permute-start = (bf16[8,256,256]{2,1,0:T(8,128)(2,1)S(1)}, bf16[8,256,256]{2,1,0:T(8,128)(2,1)}, u32[]{:S(2)}, u32[]{:S(2)}) collective-permute-start(bf16[8,256,256]{2,1,0:T(8,128)(2,1)S(1)} %slice_bitcast_fusion), channel_id=1, source_target_pairs={{0,1},{1,0},{2,3},{3,2},{4,5},{5,4},{6,7},{7,6},{8,9},{9,8},{10,11... | collective-permute-start | bytes 3145736 | tf_op jit(solution)/shard_map/ppermute | solution.py:413
  74.4 2.2 %collective-permute-start.1 = (bf16[2048,128]{1,0:T(8,128)(2,1)}, bf16[2048,128]{1,0:T(8,128)(2,1)S(1)}, u32[]{:S(2)}, u32[]{:S(2)}) collective-permute-start(bf16[2048,128]{1,0:T(8,128)(2,1)} %get-tuple-element.17), channel_id=1, source_target_pairs={{0,1},{1,0},{2,3},{3,2},{4,5},{5,4},{6,7},{7,6},{8,9},{9,8},{10,11... | collective-permute-start | bytes 1572872 | tf_op jit(solution)/shard_map/ppermute | solution.py:409
  76.6 0.8 copy-start.4
  79.6 26.4 %all-to-all-start.1 = ((bf16[8,256,256]{2,1,0:T(8,128)(2,1)}), bf16[8,256,256]{2,1,0:T(8,128)(2,1)S(1)}, u32[]{:S(2)}, u32[]{:S(2)}) async-start(bf16[8,256,256]{2,1,0:T(8,128)(2,1)} %bitcast.7), calls=%async_computation.1 | async-start | bytes 2097152 | tf_op jit(solution)/shard_map/all_to_all | solution.py:404
  100.9 2.1 %collective-permute-start.2 = (bf16[2048,128]{1,0:T(8,128)(2,1)}, bf16[2048,128]{1,0:T(8,128)(2,1)S(1)}, u32[]{:S(2)}, u32[]{:S(2)}) collective-permute-start(bf16[2048,128]{1,0:T(8,128)(2,1)} %get-tuple-element.24), channel_id=1, source_target_pairs={{0,1},{1,0},{2,3},{3,2},{4,5},{5,4},{6,7},{7,6},{8,9},{9,8},{10,11... | collective-permute-start | bytes 1572872 | tf_op jit(solution)/shard_map/ppermute | solution.py:409
  103.1 0.8 copy-start.3
  106.0 7.0 %copy-start.1 = (bf16[8,256,256]{2,1,0:T(8,128)(2,1)}, bf16[8,256,256]{2,1,0:T(8,128)(2,1)S(1)}, u32[]{:S(2)}) copy-start(bf16[8,256,256]{2,1,0:T(8,128)(2,1)S(1)} %all-to-all-done.1.in_ref) | copy-start | bytes 3145732
  106.1 22.8 %all-to-all-start.2 = ((bf16[8,256,256]{2,1,0:T(8,128)(2,1)}), bf16[8,256,256]{2,1,0:T(8,128)(2,1)S(1)}, u32[]{:S(2)}, u32[]{:S(2)}) async-start(bf16[8,256,256]{2,1,0:T(8,128)(2,1)} %bitcast.6), calls=%async_computation.2 | async-start | bytes 2097152 | tf_op jit(solution)/shard_map/all_to_all | solution.py:404
  128.9 1.0 copy-start.2

commit v3 on v0

v3 whole, which is shorter than its diff:
```python
import functools

import jax
import jax.numpy as jnp
from jax import lax
from jax.experimental import pallas as pl
from jax.experimental.pallas import tpu as pltpu
from jax.sharding import PartitionSpec as P

HEAD = 128
HEADS = 8
SCALE = HEAD**-0.5
LOG2E = 1.4426950408889634
F32 = jnp.float32
BF16 = jnp.bfloat16
NN = (((1,), (0,)), ((), ()))
NT = (((1,), (1,)), ((), ()))
VMEM_LIMIT = 46 * 2**20
SMALL = 8 * 2**20
ANY = pl.BlockSpec(memory_space=pl.ANY)
VMEM = pl.BlockSpec(memory_space=pltpu.VMEM)


def dot(a, b, dims):
    return lax.dot_general(a, b, dims, preferred_element_type=F32)


def rows(i, size):
    return pl.ds(pl.multiple_of(i * size, size), size)


def lanes(shape):
    return lax.broadcasted_iota(jnp.int32, shape, 1)


def attention_kernel(*refs):
    chunks = refs[11].shape[0]
    for step in range(2 * chunks):
        attention_step(step, *refs)


def when(condition):
    if isinstance(condition, bool):
        return (lambda f: f()) if condition else (lambda f: None)
    return pl.when(condition)


def attention_step(
    step,
    got_ref,
    far_ref,
    out_ref,
    far_out_ref,
    kk_ref,
    vt_ref,
    kt_ref,
    va_ref,
    q2_ref,
    m_ref,
    total_ref,
    e_ref,
    grad_ref,
    grad_over_ref,
    query_over_ref,
):
    blocks, _, tokens, _ = got_ref.shape
    half = blocks * tokens
    chunks, key_block, queries = e_ref.shape
    half_chunks = chunks // 2
    per_chunk = key_block // tokens
    ones = jnp.ones((8, HEAD), BF16)

    def span(i):
        return slice(i * key_block, (i + 1) * key_block) if isinstance(i, int) else rows(i, key_block)

    def scores(i):
        return dot(kk_ref[span(i), :], q2_ref[...], NT)

    def weigh(i):
        e = jnp.exp2(scores(i) - m_ref[...]).astype(BF16)
        e_ref[i] = e
        total_ref[...] += dot(vt_ref[:, span(i)], e, NN)

    @when(step == 0)
    def _():
        def prepare(load, base, top):
            def chunk(i, top):
                pair = load(pl.ds(i * per_chunk, per_chunk)).reshape(key_block, 2 * HEAD)
                k = pair[:, 0:HEAD]
                to = rows(i + base, key_block)
                kk_ref[to, 0:HEAD] = k
                kk_ref[to, HEAD : 2 * HEAD] = k
                vt_ref[0:HEAD, to] = pair[:, HEAD : 2 * HEAD].T
                vt_ref[HEAD : HEAD + 16, to] = jnp.ones((16, key_block), BF16)
                return jnp.maximum(top, dot(ones, k * k, NT))

            return lax.fori_loop(0, half_chunks, chunk, top)

        top = jnp.zeros((8, key_block), F32)
        top = prepare(lambda at: got_ref[at, 1], 0, top)
        top = prepare(lambda at: far_ref[at], half_chunks, top)
        top = jnp.max(top, axis=1, keepdims=True)[0:1, :]
        for i in range(blocks):
            to = slice(i * tokens, (i + 1) * tokens)
            q = got_ref[i, 0, :, 0:HEAD]
            scaled = q.astype(F32) * (SCALE * LOG2E)
            high = scaled.astype(BF16)
            q2_ref[to, 0:HEAD] = high
            q2_ref[to, HEAD : 2 * HEAD] = (scaled - high.astype(F32)).astype(BF16)
            size = dot(ones, q * q, NT)[0:1, :]
            m_ref[:, to] = jnp.sqrt(size * top) * (1.01 * SCALE * LOG2E)
        total_ref[...] = jnp.zeros_like(total_ref)
        lane = lanes((key_block, HEAD))
        va_ref[:, HEAD : 2 * HEAD] = jnp.where(lane < 2, 1.0, 0.0).astype(BF16)

    @when(step < chunks)
    def _():
        weigh(step)

    @when(step == chunks)
    def _():
        @when(jnp.min(total_ref[HEAD : HEAD + 1, :]) < 2.0**-80)
        def _():
            def chunk(i, top):
                s = scores(i).reshape(key_block // 8, 8, queries)
                return jnp.maximum(top, jnp.max(s, axis=0))

            top = lax.fori_loop(0, chunks, chunk, jnp.full((8, queries), -jnp.inf, F32))
            m_ref[...] = jnp.max(top, axis=0, keepdims=True)
            total_ref[...] = jnp.zeros_like(total_ref)

            def again(i, _):
                weigh(i)
                return 0

            lax.fori_loop(0, chunks, again, 0)

        inverse = 1.0 / total_ref[HEAD : HEAD + 1, :]
        m_ref[...] = inverse
        for i in range(blocks):
            to = slice(i * tokens, (i + 1) * tokens)
            part = jnp.broadcast_to(inverse[:, to], (HEAD, tokens))
            attended = (total_ref[0:HEAD, to] * part).T.astype(BF16)
            out_ref[i, 0, :, 0:HEAD] = attended
            column = part.T
            grad = got_ref[i, 0, :, HEAD : 2 * HEAD]
            grad_wide = grad.astype(F32)
            dots = jnp.sum(grad_wide * attended.astype(F32), axis=1, keepdims=True)
            dots_high = dots.astype(BF16).astype(F32)
            lane = lanes((tokens, HEAD))
            grad_ref[to, 0:HEAD] = grad
            grad_ref[to, HEAD : 2 * HEAD] = jnp.where(
                lane == 0, -dots_high, jnp.where(lane == 1, dots_high - dots, 0.0)
            ).astype(BF16)
            grad_over_ref[to, :] = (grad_wide * column).astype(BF16)
            q = got_ref[i, 0, :, 0:HEAD].astype(F32)
            query_over_ref[to, :] = (q * (column * SCALE)).astype(BF16)
        total_ref[...] = jnp.zeros_like(total_ref)

    @when(step >= chunks)
    def _():
        i = step - chunks
        is_far = i < half_chunks
        at = pl.ds(i % half_chunks * per_chunk, per_chunk)

        def take(pair):
            pair = pair.reshape(key_block, 2 * HEAD)
            kt_ref[...] = pair[:, 0:HEAD].T
            va_ref[:, 0:HEAD] = pair[:, HEAD : 2 * HEAD]

        @when(is_far)
        def _():
            take(far_ref[at])

        @when(not is_far)
        def _():
            take(got_ref[at, 1])

        e = e_ref[(i + half_chunks) % chunks]
        dv = dot(e, grad_over_ref[...], NN).astype(BF16)
        g = (e.astype(F32) * dot(va_ref[...], grad_ref[...], NT)).astype(BF16)
        dk = dot(g, query_over_ref[...], NN).astype(BF16)
        total_ref[0:HEAD, :] += dot(kt_ref[...], g, NN)

        if is_far:
            far_out_ref[span(i), 0:HEAD] = dk
            far_out_ref[span(i), HEAD : 2 * HEAD] = dv
        else:
            to = slice((i - half_chunks) * per_chunk, (i - half_chunks + 1) * per_chunk)
            out_ref[to, 1, :, 0:HEAD] = dk.reshape(per_chunk, tokens, HEAD)
            out_ref[to, 1, :, HEAD : 2 * HEAD] = dv.reshape(per_chunk, tokens, HEAD)

    @when(step == 2 * chunks - 1)
    def _():
        for i in range(blocks):
            to = slice(i * tokens, (i + 1) * tokens)
            scaled = total_ref[0:HEAD, to] * (m_ref[:, to] * SCALE)
            out_ref[i, 0, :, HEAD : 2 * HEAD] = scaled.T.astype(BF16)


def attention(got, far, key_block=1024):
    blocks, _, tokens, _ = got.shape
    half = blocks * tokens
    keys = 2 * half
    chunks = keys // key_block
    return pl.pallas_call(
        attention_kernel,
        in_specs=[VMEM, VMEM],
        out_specs=(VMEM, VMEM),
        out_shape=(
            jax.ShapeDtypeStruct(got.shape, BF16),
            jax.ShapeDtypeStruct((half, 2 * HEAD), BF16),
        ),
        scratch_shapes=[
            pltpu.VMEM((keys, 2 * HEAD), BF16),
            pltpu.VMEM((HEAD + 16, keys), BF16),
            pltpu.VMEM((HEAD, key_block), BF16),
            pltpu.VMEM((key_block, 2 * HEAD), BF16),
            pltpu.VMEM((half, 2 * HEAD), BF16),
            pltpu.VMEM((1, half), F32),
            pltpu.VMEM((HEAD + 16, half), F32),
            pltpu.VMEM((chunks, key_block, half), BF16),
            pltpu.VMEM((half, 2 * HEAD), BF16),
            pltpu.VMEM((half, HEAD), BF16),
            pltpu.VMEM((half, HEAD), BF16),
        ],
        compiler_params=pltpu.CompilerParams(vmem_limit_bytes=VMEM_LIMIT),
        cost_estimate=pl.CostEstimate(
            flops=12 * half * keys * HEAD,
            bytes_accessed=12 * half * HEAD,
            transcendentals=half * keys,
        ),
        name="attention",
    )(got, far)


def pack_kernel(q_ref, k_ref, v_ref, g_ref, out_ref, buffer, in_sem, out_sem):
    sources = (q_ref, g_ref, k_ref, v_ref)
    loads = [
        pltpu.make_async_copy(ref, buffer.at[i], in_sem.at[i]) for i, ref in enumerate(sources)
    ]
    for load in loads:
        load.start()
    stores = []
    for i, load in enumerate(loads):
        load.wait()
        for h in range(HEADS):
            store = pltpu.make_async_copy(
                buffer.at[i, :, h * HEAD : (h + 1) * HEAD],
                out_ref.at[h, i // 2, :, (i % 2) * HEAD : (i % 2 + 1) * HEAD],
                out_sem.at[i, h],
            )
            store.start()
            stores.append(store)
    for store in stores:
        store.wait()


def pack(queries, keys, values, grad_out):
    tokens = queries.shape[0]
    return pl.pallas_call(
        pack_kernel,
        in_specs=[ANY] * 4,
        out_specs=ANY,
        out_shape=jax.ShapeDtypeStruct((HEADS, 2, tokens, 2 * HEAD), BF16),
        scratch_shapes=[
            pltpu.VMEM((4, tokens, HEADS * HEAD), BF16),
            pltpu.SemaphoreType.DMA((5,)),
            pltpu.SemaphoreType.DMA((4, HEADS)),
        ],
        name="pack",
    )(queries, keys, values, grad_out)


def join_kernel(in_ref, far_ref, out_ref):
    blocks, _, tokens, _ = in_ref.shape
    out_ref[:, 0] = in_ref[:, 0]
    for i in range(blocks):
        near = in_ref[i, 1].astype(F32)
        far = far_ref[i * tokens : (i + 1) * tokens, :].astype(F32)
        out_ref[i, 1] = (near + far).astype(BF16)


def join(out, far):
    return pl.pallas_call(
        join_kernel,
        in_specs=[VMEM] * 2,
        out_specs=VMEM,
        out_shape=jax.ShapeDtypeStruct(out.shape, BF16),
        compiler_params=pltpu.CompilerParams(vmem_limit_bytes=SMALL),
        name="join",
    )(out, far)


def unpack_kernel(in_ref, *refs):
    *outs, sem = refs
    stores = [
        pltpu.make_async_copy(
            in_ref.at[h, i // 2, :, (i % 2) * HEAD : (i % 2 + 1) * HEAD],
            ref.at[:, h * HEAD : (h + 1) * HEAD],
            sem.at[i, h],
        )
        for i, ref in enumerate(outs)
        for h in range(HEADS)
    ]
    for store in stores:
        store.start()
    for store in stores:
        store.wait()


def unpack(packed):
    tokens = packed.shape[2]
    whole = jax.ShapeDtypeStruct((tokens, HEADS * HEAD), BF16)
    return pl.pallas_call(
        unpack_kernel,
        in_specs=[VMEM],
        out_specs=(ANY,) * 4,
        out_shape=(whole,) * 4,
        scratch_shapes=[pltpu.SemaphoreType.DMA((4, HEADS))],
        compiler_params=pltpu.CompilerParams(vmem_limit_bytes=SMALL),
        name="unpack",
    )(packed)


def on_device(queries, keys, values, grad_out):
    members = lax.axis_size("ctx")
    same_core = [list(range(core, members, 2)) for core in range(2)]
    other_core = [(i, i ^ 1) for i in range(members)]

    def swap(array):
        return lax.all_to_all(
            array, "ctx", 0, 0, tiled=True, axis_index_groups=same_core
        )

    def other(array):
        return lax.ppermute(array, "ctx", other_core)

    got = swap(pack(queries, keys, values, grad_out))
    out, far = attention(got, other(got[:, 1]))
    return tuple(unpack(swap(join(out, other(far)))))


def solution(mesh):
    spec = P(("dp", "ctx"), None)
    return jax.shard_map(
        on_device,
        mesh=mesh,
        in_specs=(spec,) * 4,
        out_specs=(spec,) * 4,
        check_vma=False,
    )
```

time: 543 us -> 117 us (0.22)
  waiting for transfers between devices: 334 us -> 5.17 us
  matrix products: 84.2 us -> 0 us
  blocking collectives: 0 us -> 67.6 us
  local copies, waits for them, and re-layouts: 60.5 us -> 0.07 us
  other arithmetic: 49.1 us -> 0 us
  Pallas kernels: 0 us -> 42.6 us
  between operations: 13.8 us -> 0.84 us
    reduce_scatter x1 -> x0, waiting for transfers between devices: 230 us -> none  [on_device(): lax.psum_scatter(jnp.concatenate([key_part.reshape(lax.axis_size('ctx') *...]
    all_gather x2 -> x0, waiting for transfers between devices: 104 us -> none  [the longest x1 78 us: on_device(): lax.all_gather(keys, 'ctx', axis=0, tiled=True)]
    dot_general x6 -> x0, matrix products: 84.2 us -> none  [the longest x1 17.1 us: on_device(): jnp.einsum('qhd,khd->hqk', query_heads, key_heads, preferred_element_type...]
    all_to_all x0 -> x2, blocking collectives: none -> 67.6 us  [swap(): lax.all_to_all(array, 'ctx', 0, 0, tiled=True, axis_index_groups=same_core)]
    pallas_call x0 -> x4, Pallas kernels: none -> 42.6 us  [the longest x1 38 us: attention(): pl.pallas_call(attention_kernel, in_specs=[VMEM, VMEM], out_specs=(VMEM,...]
    reshape x3 -> x0, local copies, waits for them, and re-layouts: 36.1 us -> none  [the longest x1 17.5 us: on_device(): value_part.reshape(lax.axis_size('ctx') * local_rows, features)]
    concatenate x1 -> x0, other arithmetic: 23.1 us -> none  [on_device(): jnp.concatenate([key_part.reshape(lax.axis_size('ctx') * local_rows, feat...]
    reduce_sum x1 -> x0, other arithmetic: 15.3 us -> none  [on_device(): jnp.sum(jnp.exp(scores - row_max), axis=2, keepdims=True)]
  transfers between devices with their start and end apart: 3 -> 2, of which waited for: 3 -> 2; matrix products, arithmetic and copies ran while one was open for 11% -> 0% of each run, Pallas kernels for 0% -> 0%
where the time goes in v3:
time: 117 us
  blocking collectives  67.6 us (58%)
  Pallas kernels  42.6 us (36%)
  waiting for transfers between devices  5.17 us (4%)
    all_to_all x2, blocking collectives, swap(): lax.all_to_all(array, 'ctx', 0, 0, tiled=True, axis_index_groups=same_core)  67.6 us
    pallas_call x1, Pallas kernels, attention(): pl.pallas_call(attention_kernel, in_specs=[VMEM, VMEM], out_specs=(VMEM,...  38 us
    ppermute x2, waiting for transfers between devices, other(): return lax.ppermute(array, 'ctx', other_core)  5.17 us
    pallas_call x1, Pallas kernels, pack(): pl.pallas_call(pack_kernel, in_specs=[ANY] * 4, out_specs=ANY, out_shape=...  2.71 us
  transfers between devices with their start and end apart: 2, of which 2 were waited for; matrix products, arithmetic and copies ran while one was open for 0% of the time, Pallas kernels for 0%

profile of v3, /device:TPU:0, one launch (start us, length us, event | category | flops | bytes accessed | tf_op | source)
XLA Modules:
  0.0 116.6 jit_solution(5417584825076375036)
XLA Ops:
  0.6 2.7 %pack.1 = bf16[8,2,256,256]{3,2,1,0:T(8,128)(2,1)} custom-call(bf16[256,1024]{1,0:T(8,128)(2,1)} %q_ref.1, bf16[256,1024]{1,0:T(8,128)(2,1)} %k_ref.1, bf16[256,1024]{1,0:T(8,128)(2,1)} %v_ref.1, bf16[256,1024]{1,0:T(8,128)(2,1)} %g_ref.1), custom_call_target="tpu_custom_call" | custom-call | tf_op jit(solution)/shard_map/pack/pallas_call | solution.py:261
  3.3 36.2 %all_to_all.10.refs_0_ = bf16[8,2,256,256]{3,2,1,0:T(8,128)(2,1)S(1)} all-to-all(bf16[8,2,256,256]{3,2,1,0:T(8,128)(2,1)} %pack.1), channel_id=1, replica_groups={{0,2,4,6,8,10,12,14},{1,3,5,7,9,11,13,15},{16,18,20,22,24,26,28,30},{17..., dimensions={0} | all-to-all | bytes 4194304 | tf_op jit(solution)/shard_map/all_to_all | solution.py:332
  39.6 0.1 slice_bitcast_fusion
  39.7 0.1 collective-permute-start
  39.8 2.6 %collective-permute-done.refs_1_ = bf16[8,256,256]{2,1,0:T(8,128)(2,1)S(1)} collective-permute-done((bf16[8,256,256]{2,1,0:T(8,128)(2,1)S(1)}, bf16[8,256,256]{2,1,0:T(8,128)(2,1)S(1)}, u32[]{:S(2)}, u32[]{:S(2)}) %collective-permute-start) | collective-permute-done | bytes 1048608 | tf_op jit(solution)/shard_map/ppermute | solution.py:337
  42.4 38.0 %attention.1 = (bf16[8,2,256,256]{3,2,1,0:T(8,128)(2,1)S(1)}, bf16[2048,256]{1,0:T(8,128)(2,1)S(1)}) custom-call(bf16[8,2,256,256]{3,2,1,0:T(8,128)(2,1)S(1)} %all_to_all.10.refs_0_, bf16[8,256,256]{2,1,0:T(8,128)(2,1)S(1)} %collective-permute-done.refs_1_), custom_call_target="tpu_custom_call" | custom-call | flops 12884901888 | bytes 3145728 | tf_op jit(solution)/shard_map/attention/pallas_call | solution.py:206
  80.4 0.2 collective-permute-start.1
  80.6 2.5 %collective-permute-done.1.far_ref = bf16[2048,256]{1,0:T(8,128)(2,1)S(1)} collective-permute-done((bf16[2048,256]{1,0:T(8,128)(2,1)S(1)}, bf16[2048,256]{1,0:T(8,128)(2,1)S(1)}, u32[]{:S(2)}, u32[]{:S(2)}) %collective-permute-start.1) | collective-permute-done | bytes 1048608 | tf_op jit(solution)/shard_map/ppermute | solution.py:337
  83.2 0.3 join.1
  83.5 31.4 %all_to_all.11.in_ref = bf16[8,2,256,256]{3,2,1,0:T(8,128)(2,1)S(1)} all-to-all(bf16[8,2,256,256]{3,2,1,0:T(8,128)(2,1)S(1)} %join.1), channel_id=1, replica_groups={{0,2,4,6,8,10,12,14},{1,3,5,7,9,11,13,15},{16,18,20,22,24,26,28,30},{17..., dimensions={0} | all-to-all | bytes 4194304 | tf_op jit(solution)/shard_map/all_to_all | solution.py:332
  114.9 1.6 %unpack.1 = (bf16[256,1024]{1,0:T(8,128)(2,1)}, bf16[256,1024]{1,0:T(8,128)(2,1)}, bf16[256,1024]{1,0:T(8,128)(2,1)}, bf16[256,1024]{1,0:T(8,128)(2,1)}) custom-call(bf16[8,2,256,256]{3,2,1,0:T(8,128)(2,1)S(1)} %all_to_all.11.in_ref), custom_call_target="tpu_custom_call" | custom-call | tf_op jit(solution)/shard_map/unpack/pallas_call | solution.py:315
Async XLA Ops:
  39.7 2.7 %collective-permute-start = (bf16[8,256,256]{2,1,0:T(8,128)(2,1)S(1)}, bf16[8,256,256]{2,1,0:T(8,128)(2,1)S(1)}, u32[]{:S(2)}, u32[]{:S(2)}) collective-permute-start(bf16[8,256,256]{2,1,0:T(8,128)(2,1)S(1)} %slice_bitcast_fusion), channel_id=1, source_target_pairs={{0,1},{1,0},{2,3},{3,2},{4,5},{5,4},{6,7},{7,6},{8,9},{9,8},{10,11... | collective-permute-start | bytes 3145736 | tf_op jit(solution)/shard_map/ppermute | solution.py:337
  80.4 2.7 %collective-permute-start.1 = (bf16[2048,256]{1,0:T(8,128)(2,1)S(1)}, bf16[2048,256]{1,0:T(8,128)(2,1)S(1)}, u32[]{:S(2)}, u32[]{:S(2)}) collective-permute-start(bf16[2048,256]{1,0:T(8,128)(2,1)S(1)} %get-tuple-element.7), channel_id=1, source_target_pairs={{0,1},{1,0},{2,3},{3,2},{4,5},{5,4},{6,7},{7,6},{8,9},{9,8},{10,11... | collective-permute-start | bytes 3145736 | tf_op jit(solution)/shard_map/ppermute | solution.py:337

commit v4 on v3

--- a/solution.py
+++ b/solution.py
@@ -19,6 +19,13 @@
 SMALL = 8 * 2**20
 ANY = pl.BlockSpec(memory_space=pl.ANY)
 VMEM = pl.BlockSpec(memory_space=pltpu.VMEM)
+ROW = 4
+HOPS = ((0, 0), (1, 2), (1, 1), (1, 3), (1, 0), (0, 2), (0, 1), (0, 3))
+
+
+def chip_at(chip, hop, sign=1):
+    x, z = chip // ROW, chip % ROW
+    return (x + hop[0]) % 2 * ROW + (z + sign * hop[1] + ROW) % ROW
 
 
 def dot(a, b, dims):
@@ -34,9 +41,10 @@
 
 
 def attention_kernel(*refs):
-    chunks = refs[11].shape[0]
+    got, refs = refs[:HEADS], refs[HEADS:]
+    chunks = refs[10].shape[0]
     for step in range(2 * chunks):
-        attention_step(step, *refs)
+        attention_step(step, got, *refs)
 
 
 def when(condition):
@@ -47,7 +55,7 @@
 
 def attention_step(
     step,
-    got_ref,
+    got,
     far_ref,
     out_ref,
     far_out_ref,
@@ -63,7 +71,8 @@
     grad_over_ref,
     query_over_ref,
 ):
-    blocks, _, tokens, _ = got_ref.shape
+    blocks = len(got)
+    tokens = got[0].shape[1]
     half = blocks * tokens
     chunks, key_block, queries = e_ref.shape
     half_chunks = chunks // 2
@@ -83,26 +92,20 @@
 
     @when(step == 0)
     def _():
-        def prepare(load, base, top):
-            def chunk(i, top):
-                pair = load(pl.ds(i * per_chunk, per_chunk)).reshape(key_block, 2 * HEAD)
-                k = pair[:, 0:HEAD]
-                to = rows(i + base, key_block)
-                kk_ref[to, 0:HEAD] = k
-                kk_ref[to, HEAD : 2 * HEAD] = k
-                vt_ref[0:HEAD, to] = pair[:, HEAD : 2 * HEAD].T
-                vt_ref[HEAD : HEAD + 16, to] = jnp.ones((16, key_block), BF16)
-                return jnp.maximum(top, dot(ones, k * k, NT))
-
-            return lax.fori_loop(0, half_chunks, chunk, top)
-
-        top = jnp.zeros((8, key_block), F32)
-        top = prepare(lambda at: got_ref[at, 1], 0, top)
-        top = prepare(lambda at: far_ref[at], half_chunks, top)
+        top = jnp.zeros((8, tokens), F32)
+        for i in range(2 * blocks):
+            pair = got[i][1] if i < blocks else far_ref[i - blocks]
+            k = pair[:, 0:HEAD]
+            to = slice(i * tokens, (i + 1) * tokens)
+            kk_ref[to, 0:HEAD] = k
+            kk_ref[to, HEAD : 2 * HEAD] = k
+            vt_ref[0:HEAD, to] = pair[:, HEAD : 2 * HEAD].T
+            vt_ref[HEAD : HEAD + 16, to] = jnp.ones((16, tokens), BF16)
+            top = jnp.maximum(top, dot(ones, k * k, NT))
         top = jnp.max(top, axis=1, keepdims=True)[0:1, :]
         for i in range(blocks):
             to = slice(i * tokens, (i + 1) * tokens)
-            q = got_ref[i, 0, :, 0:HEAD]
+            q = got[i][0, :, 0:HEAD]
             scaled = q.astype(F32) * (SCALE * LOG2E)
             high = scaled.astype(BF16)
             q2_ref[to, 0:HEAD] = high
@@ -143,7 +146,7 @@
             attended = (total_ref[0:HEAD, to] * part).T.astype(BF16)
             out_ref[i, 0, :, 0:HEAD] = attended
             column = part.T
-            grad = got_ref[i, 0, :, HEAD : 2 * HEAD]
+            grad = got[i][0, :, HEAD : 2 * HEAD]
             grad_wide = grad.astype(F32)
             dots = jnp.sum(grad_wide * attended.astype(F32), axis=1, keepdims=True)
             dots_high = dots.astype(BF16).astype(F32)
@@ -153,7 +156,7 @@
                 lane == 0, -dots_high, jnp.where(lane == 1, dots_high - dots, 0.0)
             ).astype(BF16)
             grad_over_ref[to, :] = (grad_wide * column).astype(BF16)
-            q = got_ref[i, 0, :, 0:HEAD].astype(F32)
+            q = got[i][0, :, 0:HEAD].astype(F32)
             query_over_ref[to, :] = (q * (column * SCALE)).astype(BF16)
         total_ref[...] = jnp.zeros_like(total_ref)
 
@@ -161,20 +164,12 @@
     def _():
         i = step - chunks
         is_far = i < half_chunks
-        at = pl.ds(i % half_chunks * per_chunk, per_chunk)
-
-        def take(pair):
-            pair = pair.reshape(key_block, 2 * HEAD)
-            kt_ref[...] = pair[:, 0:HEAD].T
-            va_ref[:, 0:HEAD] = pair[:, HEAD : 2 * HEAD]
-
-        @when(is_far)
-        def _():
-            take(far_ref[at])
-
-        @when(not is_far)
-        def _():
-            take(got_ref[at, 1])
+        for j in range(per_chunk):
+            block = i % half_chunks * per_chunk + j
+            pair = far_ref[block] if is_far else got[block][1]
+            to = slice(j * tokens, (j + 1) * tokens)
+            kt_ref[:, to] = pair[:, 0:HEAD].T
+            va_ref[to, 0:HEAD] = pair[:, HEAD : 2 * HEAD]
 
         e = e_ref[(i + half_chunks) % chunks]
         dv = dot(e, grad_over_ref[...], NN).astype(BF16)
@@ -199,16 +194,16 @@
 
 
 def attention(got, far, key_block=1024):
-    blocks, _, tokens, _ = got.shape
+    blocks, tokens = len(got), got[0].shape[1]
     half = blocks * tokens
     keys = 2 * half
     chunks = keys // key_block
     return pl.pallas_call(
         attention_kernel,
-        in_specs=[VMEM, VMEM],
+        in_specs=[VMEM] * (blocks + 1),
         out_specs=(VMEM, VMEM),
         out_shape=(
-            jax.ShapeDtypeStruct(got.shape, BF16),
+            jax.ShapeDtypeStruct((blocks, 2, tokens, 2 * HEAD), BF16),
             jax.ShapeDtypeStruct((half, 2 * HEAD), BF16),
         ),
         scratch_shapes=[
@@ -231,10 +226,12 @@
             transcendentals=half * keys,
         ),
         name="attention",
-    )(got, far)
-
-
-def pack_kernel(q_ref, k_ref, v_ref, g_ref, out_ref, buffer, in_sem, out_sem):
+    )(*got, far)
+
+
+def pack_kernel(q_ref, k_ref, v_ref, g_ref, *refs):
+    outs, (buffer, in_sem, out_sem) = refs[:HEADS], refs[HEADS:]
+    chip = lax.axis_index("ctx") // 2
     sources = (q_ref, g_ref, k_ref, v_ref)
     loads = [
         pltpu.make_async_copy(ref, buffer.at[i], in_sem.at[i]) for i, ref in enumerate(sources)
@@ -244,11 +241,12 @@
     stores = []
     for i, load in enumerate(loads):
         load.wait()
-        for h in range(HEADS):
+        for j, hop in enumerate(HOPS):
+            head = pl.multiple_of(chip_at(chip, hop) * HEAD, HEAD)
             store = pltpu.make_async_copy(
-                buffer.at[i, :, h * HEAD : (h + 1) * HEAD],
-                out_ref.at[h, i // 2, :, (i % 2) * HEAD : (i % 2 + 1) * HEAD],
-                out_sem.at[i, h],
+                buffer.at[i, :, pl.ds(head, HEAD)],
+                outs[j].at[i // 2, :, (i % 2) * HEAD : (i % 2 + 1) * HEAD],
+                out_sem.at[i, j],
             )
             store.start()
             stores.append(store)
@@ -261,84 +259,106 @@
     return pl.pallas_call(
         pack_kernel,
         in_specs=[ANY] * 4,
-        out_specs=ANY,
-        out_shape=jax.ShapeDtypeStruct((HEADS, 2, tokens, 2 * HEAD), BF16),
+        out_specs=(ANY,) * HEADS,
+        out_shape=(jax.ShapeDtypeStruct((2, tokens, 2 * HEAD), BF16),) * HEADS,
         scratch_shapes=[
             pltpu.VMEM((4, tokens, HEADS * HEAD), BF16),
-            pltpu.SemaphoreType.DMA((5,)),
+            pltpu.SemaphoreType.DMA((4,)),
             pltpu.SemaphoreType.DMA((4, HEADS)),
         ],
         name="pack",
     )(queries, keys, values, grad_out)
 
 
-def join_kernel(in_ref, far_ref, out_ref):
-    blocks, _, tokens, _ = in_ref.shape
-    out_ref[:, 0] = in_ref[:, 0]
-    for i in range(blocks):
+def pairs_kernel(*refs):
+    *blocks, out_ref = refs
+    for i, ref in enumerate(blocks):
+        out_ref[i] = ref[1]
+
+
+def pairs(blocks):
+    _, tokens, features = blocks[0].shape
+    return pl.pallas_call(
+        pairs_kernel,
+        in_specs=[VMEM] * len(blocks),
+        out_specs=VMEM,
+        out_shape=jax.ShapeDtypeStruct((len(blocks), tokens, features), BF16),
+        compiler_params=pltpu.CompilerParams(vmem_limit_bytes=SMALL),
+        name="pairs",
+    )(*blocks)
+
+
+def join_kernel(in_ref, far_ref, *outs):
+    tokens = in_ref.shape[2]
+    for i, out_ref in enumerate(outs):
+        out_ref[0] = in_ref[i, 0]
         near = in_ref[i, 1].astype(F32)
         far = far_ref[i * tokens : (i + 1) * tokens, :].astype(F32)
-        out_ref[i, 1] = (near + far).astype(BF16)
+        out_ref[1] = (near + far).astype(BF16)
 
 
 def join(out, far):
+    blocks = out.shape[0]
     return pl.pallas_call(
         join_kernel,
         in_specs=[VMEM] * 2,
-        out_specs=VMEM,
-        out_shape=jax.ShapeDtypeStruct(out.shape, BF16),
+        out_specs=(VMEM,) * blocks,
+        out_shape=(jax.ShapeDtypeStruct(out.shape[1:], BF16),) * blocks,
         compiler_params=pltpu.CompilerParams(vmem_limit_bytes=SMALL),
         name="join",
     )(out, far)
 
 
-def unpack_kernel(in_ref, *refs):
-    *outs, sem = refs
-    stores = [
-        pltpu.make_async_copy(
-            in_ref.at[h, i // 2, :, (i % 2) * HEAD : (i % 2 + 1) * HEAD],
-            ref.at[:, h * HEAD : (h + 1) * HEAD],
-            sem.at[i, h],
-        )
-        for i, ref in enumerate(outs)
-        for h in range(HEADS)
-    ]
-    for store in stores:
-        store.start()
+def unpack_kernel(*refs):
+    blocks, outs, sem = refs[:HEADS], refs[HEADS:-1], refs[-1]
+    chip = lax.axis_index("ctx") // 2
+    stores = []
+    for j, hop in enumerate(HOPS):
+        head = pl.multiple_of(chip_at(chip, hop) * HEAD, HEAD)
+        for i, ref in enumerate(outs):
+            store = pltpu.make_async_copy(
+                blocks[j].at[i // 2, :, (i % 2) * HEAD : (i % 2 + 1) * HEAD],
+                ref.at[:, pl.ds(head, HEAD)],
+                sem.at[i, j],
+            )
+            store.start()
+            stores.append(store)
     for store in stores:
         store.wait()
 
 
-def unpack(packed):
-    tokens = packed.shape[2]
+def unpack(blocks):
+    tokens = blocks[0].shape[1]
     whole = jax.ShapeDtypeStruct((tokens, HEADS * HEAD), BF16)
     return pl.pallas_call(
         unpack_kernel,
-        in_specs=[VMEM],
+        in_specs=[VMEM] * HEADS,
         out_specs=(ANY,) * 4,
         out_shape=(whole,) * 4,
         scratch_shapes=[pltpu.SemaphoreType.DMA((4, HEADS))],
         compiler_params=pltpu.CompilerParams(vmem_limit_bytes=SMALL),
         name="unpack",
-    )(packed)
+    )(*blocks)
 
 
 def on_device(queries, keys, values, grad_out):
     members = lax.axis_size("ctx")
-    same_core = [list(range(core, members, 2)) for core in range(2)]
     other_core = [(i, i ^ 1) for i in range(members)]
-
-    def swap(array):
-        return lax.all_to_all(
-            array, "ctx", 0, 0, tiled=True, axis_index_groups=same_core
-        )
 
     def other(array):
         return lax.ppermute(array, "ctx", other_core)
 
-    got = swap(pack(queries, keys, values, grad_out))
-    out, far = attention(got, other(got[:, 1]))
-    return tuple(unpack(swap(join(out, other(far)))))
+    def travel(blocks, sign):
+        moved = [blocks[0]]
+        for block, hop in zip(blocks[1:], HOPS[1:]):
+            to = [(i, chip_at(i // 2, hop, sign) * 2 + i % 2) for i in range(members)]
+            moved.append(lax.ppermute(block, "ctx", to))
+        return moved
+
+    got = travel(pack(queries, keys, values, grad_out), 1)
+    out, far = attention(got, other(pairs(got)))
+    attended, query_grads, key_grads, value_grads = unpack(travel(join(out, other(far)), -1))
+    return attended, query_grads, key_grads, value_grads
 
 
 def solution(mesh):

time: 117 us -> 111 us (0.949)
  blocking collectives: 67.6 us -> 0 us
  waiting for transfers between devices: 5.17 us -> 36.4 us
  starting transfers between devices: 0.3 us -> 30 us
    all_to_all x2 -> x0, blocking collectives: 67.6 us -> none  [swap(): lax.all_to_all(array, 'ctx', 0, 0, tiled=True, axis_index_groups=same_core)]
    ppermute x0 -> x14, waiting for transfers between devices: none -> 31.2 us  [travel(): moved.append(lax.ppermute(block, 'ctx', to))]
    ppermute x0 -> x14, starting transfers between devices: none -> 29.7 us  [travel(): moved.append(lax.ppermute(block, 'ctx', to))]
    pallas_call x4 -> x5, Pallas kernels: 42.6 us -> 41.9 us  [the longest x1 37.4 us: attention(): pl.pallas_call(attention_kernel, in_specs=[VMEM] * (blocks + 1), out_spec...]
  transfers between devices with their start and end apart: 2 -> 16, of which waited for: 2 -> 12; matrix products, arithmetic and copies ran while one was open for 0% -> 0% of each run, Pallas kernels for 0% -> 0%
where the time goes in v4:
time: 111 us; the launch traced here: 110 us
  Pallas kernels  41.9 us (38%)
  waiting for transfers between devices  36.4 us (33%)
  starting transfers between devices  30 us (27%)
    pallas_call x1, Pallas kernels, attention(): pl.pallas_call(attention_kernel, in_specs=[VMEM] * (blocks + 1), out_spec...  37.4 us
    ppermute x14, waiting for transfers between devices, travel(): moved.append(lax.ppermute(block, 'ctx', to))  31.2 us
    ppermute x14, starting transfers between devices, travel(): moved.append(lax.ppermute(block, 'ctx', to))  29.7 us
    ppermute x2, waiting for transfers between devices, other(): return lax.ppermute(array, 'ctx', other_core)  5.16 us
    pallas_call x1, Pallas kernels, pack(): pl.pallas_call(pack_kernel, in_specs=[ANY] * 4, out_specs=(ANY,) * HEADS,...  2.64 us
  transfers between devices with their start and end apart: 16, of which 12 were waited for; matrix products, arithmetic and copies ran while one was open for 0% of the time, Pallas kernels for 0%

profile of v4, /device:TPU:0, one launch (start us, length us, event | category | flops | bytes accessed | tf_op | source)
XLA Modules:
  0.0 110.1 jit_solution(18145411824736233155)
XLA Ops:
  0.6 2.6 %pack.1 = (bf16[2,256,256]{2,1,0:T(8,128)(2,1)}, bf16[2,256,256]{2,1,0:T(8,128)(2,1)}, bf16[2,256,256]{2,1,0:T(8,128)(2,1)}, bf16[2,256,256]{2,1,0:T(8,128)(2,1)...) custom-call(bf16[256,1024]{1,0:T(8,128)(2,1)} %q_ref.1, ...), custom_call_target="tpu_custom_call" | custom-call | tf_op jit(solution)/shard_map/pack/pallas_call | solution.py:259
  3.3 6.5 %collective-permute-start = (bf16[2,256,256]{2,1,0:T(8,128)(2,1)}, bf16[2,256,256]{2,1,0:T(8,128)(2,1)S(1)}, u32[]{:S(2)}, u32[]{:S(2)}) collective-permute-start(bf16[2,256,256]{2,1,0:T(8,128)(2,1)} %get-tuple-element.23), channel_id=1, source_target_pairs={{0,12},{1,13},{2,14},{3,15},{4,8},{5,9},{6,10},{7,11},{8,4},{9,5},... | collective-permute-start | bytes 786440 | tf_op jit(solution)/shard_map/ppermute | solution.py:355
  9.8 1.0 collective-permute-start.1
  10.7 4.7 %collective-permute-start.2 = (bf16[2,256,256]{2,1,0:T(8,128)(2,1)}, bf16[2,256,256]{2,1,0:T(8,128)(2,1)S(1)}, u32[]{:S(2)}, u32[]{:S(2)}) collective-permute-start(bf16[2,256,256]{2,1,0:T(8,128)(2,1)} %get-tuple-element.25), channel_id=1, source_target_pairs={{0,14},{1,15},{2,8},{3,9},{4,10},{5,11},{6,12},{7,13},{8,6},{9,7},... | collective-permute-start | bytes 786440 | tf_op jit(solution)/shard_map/ppermute | solution.py:355
  15.4 0.5 collective-permute-start.3
  15.9 1.2 %collective-permute-done.refs_1_ = bf16[2,256,256]{2,1,0:T(8,128)(2,1)S(1)} collective-permute-done((bf16[2,256,256]{2,1,0:T(8,128)(2,1)}, bf16[2,256,256]{2,1,0:T(8,128)(2,1)S(1)}, u32[]{:S(2)}, u32[]{:S(2)}) %collective-permute-start) | collective-permute-done | bytes 262176 | tf_op jit(solution)/shard_map/ppermute | solution.py:355
  17.1 1.2 %collective-permute-start.5 = (bf16[2,256,256]{2,1,0:T(8,128)(2,1)}, bf16[2,256,256]{2,1,0:T(8,128)(2,1)S(1)}, u32[]{:S(2)}, u32[]{:S(2)}) collective-permute-start(bf16[2,256,256]{2,1,0:T(8,128)(2,1)} %get-tuple-element.28), channel_id=1, source_target_pairs={{0,2},{1,3},{2,4},{3,5},{4,6},{5,7},{6,0},{7,1},{8,10},{9,11},{10,... | collective-permute-start | bytes 786440 | tf_op jit(solution)/shard_map/ppermute | solution.py:355
  18.4 5.2 %collective-permute-done.1.refs_2_ = bf16[2,256,256]{2,1,0:T(8,128)(2,1)S(1)} collective-permute-done((bf16[2,256,256]{2,1,0:T(8,128)(2,1)}, bf16[2,256,256]{2,1,0:T(8,128)(2,1)S(1)}, u32[]{:S(2)}, u32[]{:S(2)}) %collective-permute-start.1) | collective-permute-done | bytes 262176 | tf_op jit(solution)/shard_map/ppermute | solution.py:355
  23.6 6.3 %collective-permute-done.2.refs_3_ = bf16[2,256,256]{2,1,0:T(8,128)(2,1)S(1)} collective-permute-done((bf16[2,256,256]{2,1,0:T(8,128)(2,1)}, bf16[2,256,256]{2,1,0:T(8,128)(2,1)S(1)}, u32[]{:S(2)}, u32[]{:S(2)}) %collective-permute-start.2) | collective-permute-done | bytes 262176 | tf_op jit(solution)/shard_map/ppermute | solution.py:355
  30.0 4.3 %collective-permute-done.3.refs_4_ = bf16[2,256,256]{2,1,0:T(8,128)(2,1)S(1)} collective-permute-done((bf16[2,256,256]{2,1,0:T(8,128)(2,1)}, bf16[2,256,256]{2,1,0:T(8,128)(2,1)S(1)}, u32[]{:S(2)}, u32[]{:S(2)}) %collective-permute-start.3) | collective-permute-done | bytes 262176 | tf_op jit(solution)/shard_map/ppermute | solution.py:355
  34.3 0.1 collective-permute-done.6.refs_7_
  34.4 0.9 copy-done
  35.3 0.1 pairs.1
  35.4 0.1 collective-permute-start.7
  35.5 2.6 %collective-permute-done.7.refs_8_ = bf16[8,256,256]{2,1,0:T(8,128)(2,1)S(1)} collective-permute-done((bf16[8,256,256]{2,1,0:T(8,128)(2,1)S(1)}, bf16[8,256,256]{2,1,0:T(8,128)(2,1)S(1)}, u32[]{:S(2)}, u32[]{:S(2)}) %collective-permute-start.7) | collective-permute-done | bytes 1048608 | tf_op jit(solution)/shard_map/ppermute | solution.py:349
  38.1 37.4 %attention.1 = (bf16[8,2,256,256]{3,2,1,0:T(8,128)(2,1)S(1)}, bf16[2048,256]{1,0:T(8,128)(2,1)S(1)}) custom-call(bf16[2,256,256]{2,1,0:T(8,128)(2,1)S(1)} %copy-done.1, bf16[2,256,256]{2,1,0:T(8,128)(2,1)S(1)} %collective-permute-done.refs_1_, bf16[2,256,256]{2,1,0:T(8,128)(2,1)S(1)} %collective-permute-done.1.refs_2_, ...), custom_call_target="tpu_custom_call" | custom-call | flops 12884901888 | bytes 3145728 | tf_op jit(solution)/shard_map/attention/pallas_call | solution.py:201
  75.5 0.2 collective-permute-start.8
  75.7 2.5 %collective-permute-done.8.far_ref = bf16[2048,256]{1,0:T(8,128)(2,1)S(1)} collective-permute-done((bf16[2048,256]{1,0:T(8,128)(2,1)S(1)}, bf16[2048,256]{1,0:T(8,128)(2,1)S(1)}, u32[]{:S(2)}, u32[]{:S(2)}) %collective-permute-start.8) | collective-permute-done | bytes 1048608 | tf_op jit(solution)/shard_map/ppermute | solution.py:349
  78.3 0.2 join.1
  78.5 4.7 %collective-permute-start.9 = (bf16[2,256,256]{2,1,0:T(8,128)(2,1)S(1)}, bf16[2,256,256]{2,1,0:T(8,128)(2,1)S(1)}, u32[]{:S(2)}, u32[]{:S(2)}) collective-permute-start(bf16[2,256,256]{2,1,0:T(8,128)(2,1)S(1)} %get-tuple-element.33), channel_id=1, source_target_pairs={{0,12},{1,13},{2,14},{3,15},{4,8},{5,9},{6,10},{7,11},{8,4},{9,5},... | collective-permute-start | bytes 786440 | tf_op jit(solution)/shard_map/ppermute | solution.py:355
  83.2 1.7 %collective-permute-start.10 = (bf16[2,256,256]{2,1,0:T(8,128)(2,1)S(1)}, bf16[2,256,256]{2,1,0:T(8,128)(2,1)S(1)}, u32[]{:S(2)}, u32[]{:S(2)}) collective-permute-start(bf16[2,256,256]{2,1,0:T(8,128)(2,1)S(1)} %get-tuple-element.34), channel_id=1, source_target_pairs={{0,14},{1,15},{2,8},{3,9},{4,10},{5,11},{6,12},{7,13},{8,6},{9,7},... | collective-permute-start | bytes 786440 | tf_op jit(solution)/shard_map/ppermute | solution.py:355
  84.9 2.7 %collective-permute-start.11 = (bf16[2,256,256]{2,1,0:T(8,128)(2,1)S(1)}, bf16[2,256,256]{2,1,0:T(8,128)(2,1)S(1)}, u32[]{:S(2)}, u32[]{:S(2)}) collective-permute-start(bf16[2,256,256]{2,1,0:T(8,128)(2,1)S(1)} %get-tuple-element.35), channel_id=1, source_target_pairs={{0,10},{1,11},{2,12},{3,13},{4,14},{5,15},{6,8},{7,9},{8,2},{9,3},... | collective-permute-start | bytes 786440 | tf_op jit(solution)/shard_map/ppermute | solution.py:355
  87.6 0.3 collective-permute-start.12
  87.9 1.6 %collective-permute-start.13 = (bf16[2,256,256]{2,1,0:T(8,128)(2,1)S(1)}, bf16[2,256,256]{2,1,0:T(8,128)(2,1)S(1)}, u32[]{:S(2)}, u32[]{:S(2)}) collective-permute-start(bf16[2,256,256]{2,1,0:T(8,128)(2,1)S(1)} %get-tuple-element.37), channel_id=1, source_target_pairs={{0,4},{1,5},{2,6},{3,7},{4,0},{5,1},{6,2},{7,3},{8,12},{9,13},{10,... | collective-permute-start | bytes 786440 | tf_op jit(solution)/shard_map/ppermute | solution.py:355
  89.5 2.1 %collective-permute-done.9.refs_1_ = bf16[2,256,256]{2,1,0:T(8,128)(2,1)S(1)} collective-permute-done((bf16[2,256,256]{2,1,0:T(8,128)(2,1)S(1)}, bf16[2,256,256]{2,1,0:T(8,128)(2,1)S(1)}, u32[]{:S(2)}, u32[]{:S(2)}) %collective-permute-start.9) | collective-permute-done | bytes 262176 | tf_op jit(solution)/shard_map/ppermute | solution.py:355
  91.6 3.4 %collective-permute-start.14 = (bf16[2,256,256]{2,1,0:T(8,128)(2,1)S(1)}, bf16[2,256,256]{2,1,0:T(8,128)(2,1)S(1)}, u32[]{:S(2)}, u32[]{:S(2)}) collective-permute-start(bf16[2,256,256]{2,1,0:T(8,128)(2,1)S(1)} %get-tuple-element.38), channel_id=1, source_target_pairs={{0,6},{1,7},{2,0},{3,1},{4,2},{5,3},{6,4},{7,5},{8,14},{9,15},{10,... | collective-permute-start | bytes 786440 | tf_op jit(solution)/shard_map/ppermute | solution.py:355
  95.0 2.1 %collective-permute-done.10.refs_2_ = bf16[2,256,256]{2,1,0:T(8,128)(2,1)S(1)} collective-permute-done((bf16[2,256,256]{2,1,0:T(8,128)(2,1)S(1)}, bf16[2,256,256]{2,1,0:T(8,128)(2,1)S(1)}, u32[]{:S(2)}, u32[]{:S(2)}) %collective-permute-start.10) | collective-permute-done | bytes 262176 | tf_op jit(solution)/shard_map/ppermute | solution.py:355
  97.1 1.5 %collective-permute-start.15 = (bf16[2,256,256]{2,1,0:T(8,128)(2,1)S(1)}, bf16[2,256,256]{2,1,0:T(8,128)(2,1)S(1)}, u32[]{:S(2)}, u32[]{:S(2)}) collective-permute-start(bf16[2,256,256]{2,1,0:T(8,128)(2,1)S(1)} %get-tuple-element.39), channel_id=1, source_target_pairs={{0,2},{1,3},{2,4},{3,5},{4,6},{5,7},{6,0},{7,1},{8,10},{9,11},{10,... | collective-permute-start | bytes 786440 | tf_op jit(solution)/shard_map/ppermute | solution.py:355
  98.6 4.9 %collective-permute-done.11.refs_3_ = bf16[2,256,256]{2,1,0:T(8,128)(2,1)S(1)} collective-permute-done((bf16[2,256,256]{2,1,0:T(8,128)(2,1)S(1)}, bf16[2,256,256]{2,1,0:T(8,128)(2,1)S(1)}, u32[]{:S(2)}, u32[]{:S(2)}) %collective-permute-start.11) | collective-permute-done | bytes 262176 | tf_op jit(solution)/shard_map/ppermute | solution.py:355
  103.5 4.1 %collective-permute-done.12.refs_4_ = bf16[2,256,256]{2,1,0:T(8,128)(2,1)S(1)} collective-permute-done((bf16[2,256,256]{2,1,0:T(8,128)(2,1)S(1)}, bf16[2,256,256]{2,1,0:T(8,128)(2,1)S(1)}, u32[]{:S(2)}, u32[]{:S(2)}) %collective-permute-start.12) | collective-permute-done | bytes 262176 | tf_op jit(solution)/shard_map/ppermute | solution.py:355
  107.6 0.7 collective-permute-done.15.refs_7_
  108.3 1.6 %unpack.1 = (bf16[256,1024]{1,0:T(8,128)(2,1)}, bf16[256,1024]{1,0:T(8,128)(2,1)}, bf16[256,1024]{1,0:T(8,128)(2,1)}, bf16[256,1024]{1,0:T(8,128)(2,1)}) custom-call(bf16[2,256,256]{2,1,0:T(8,128)(2,1)S(1)} %get-tuple-element.32.refs_0_, bf16[2,256,256]{2,1,0:T(8,128)(2,1)S(1)} %collective-permute-done.9.refs_1_, ...), custom_call_target="tpu_custom_call" | custom-call | tf_op jit(solution)/shard_map/unpack/pallas_call | solution.py:333
  (9 shorter events, 0.0 us)
Async XLA Ops:
  3.3 13.8 %collective-permute-start = (bf16[2,256,256]{2,1,0:T(8,128)(2,1)}, bf16[2,256,256]{2,1,0:T(8,128)(2,1)S(1)}, u32[]{:S(2)}, u32[]{:S(2)}) collective-permute-start(bf16[2,256,256]{2,1,0:T(8,128)(2,1)} %get-tuple-element.23), channel_id=1, source_target_pairs={{0,12},{1,13},{2,14},{3,15},{4,8},{5,9},{6,10},{7,11},{8,4},{9,5},... | collective-permute-start | bytes 786440 | tf_op jit(solution)/shard_map/ppermute | solution.py:355
  9.8 13.8 %collective-permute-start.1 = (bf16[2,256,256]{2,1,0:T(8,128)(2,1)}, bf16[2,256,256]{2,1,0:T(8,128)(2,1)S(1)}, u32[]{:S(2)}, u32[]{:S(2)}) collective-permute-start(bf16[2,256,256]{2,1,0:T(8,128)(2,1)} %get-tuple-element.24), channel_id=1, source_target_pairs={{0,10},{1,11},{2,12},{3,13},{4,14},{5,15},{6,8},{7,9},{8,2},{9,3},... | collective-permute-start | bytes 786440 | tf_op jit(solution)/shard_map/ppermute | solution.py:355
  10.7 19.2 %collective-permute-start.2 = (bf16[2,256,256]{2,1,0:T(8,128)(2,1)}, bf16[2,256,256]{2,1,0:T(8,128)(2,1)S(1)}, u32[]{:S(2)}, u32[]{:S(2)}) collective-permute-start(bf16[2,256,256]{2,1,0:T(8,128)(2,1)} %get-tuple-element.25), channel_id=1, source_target_pairs={{0,14},{1,15},{2,8},{3,9},{4,10},{5,11},{6,12},{7,13},{8,6},{9,7},... | collective-permute-start | bytes 786440 | tf_op jit(solution)/shard_map/ppermute | solution.py:355
  15.4 18.8 %collective-permute-start.3 = (bf16[2,256,256]{2,1,0:T(8,128)(2,1)}, bf16[2,256,256]{2,1,0:T(8,128)(2,1)S(1)}, u32[]{:S(2)}, u32[]{:S(2)}) collective-permute-start(bf16[2,256,256]{2,1,0:T(8,128)(2,1)} %get-tuple-element.26), channel_id=1, source_target_pairs={{0,8},{1,9},{2,10},{3,11},{4,12},{5,13},{6,14},{7,15},{8,0},{9,1},... | collective-permute-start | bytes 786440 | tf_op jit(solution)/shard_map/ppermute | solution.py:355
  15.9 18.3 %collective-permute-start.4 = (bf16[2,256,256]{2,1,0:T(8,128)(2,1)}, bf16[2,256,256]{2,1,0:T(8,128)(2,1)S(1)}, u32[]{:S(2)}, u32[]{:S(2)}) collective-permute-start(bf16[2,256,256]{2,1,0:T(8,128)(2,1)} %get-tuple-element.27), channel_id=1, source_target_pairs={{0,4},{1,5},{2,6},{3,7},{4,0},{5,1},{6,2},{7,3},{8,12},{9,13},{10,... | collective-permute-start | bytes 786440 | tf_op jit(solution)/shard_map/ppermute | solution.py:355
  17.1 17.1 %collective-permute-start.5 = (bf16[2,256,256]{2,1,0:T(8,128)(2,1)}, bf16[2,256,256]{2,1,0:T(8,128)(2,1)S(1)}, u32[]{:S(2)}, u32[]{:S(2)}) collective-permute-start(bf16[2,256,256]{2,1,0:T(8,128)(2,1)} %get-tuple-element.28), channel_id=1, source_target_pairs={{0,2},{1,3},{2,4},{3,5},{4,6},{5,7},{6,0},{7,1},{8,10},{9,11},{10,... | collective-permute-start | bytes 786440 | tf_op jit(solution)/shard_map/ppermute | solution.py:355
  23.6 10.8 %collective-permute-start.6 = (bf16[2,256,256]{2,1,0:T(8,128)(2,1)}, bf16[2,256,256]{2,1,0:T(8,128)(2,1)S(1)}, u32[]{:S(2)}, u32[]{:S(2)}) collective-permute-start(bf16[2,256,256]{2,1,0:T(8,128)(2,1)} %get-tuple-element.29), channel_id=1, source_target_pairs={{0,6},{1,7},{2,0},{3,1},{4,2},{5,3},{6,4},{7,5},{8,14},{9,15},{10,... | collective-permute-start | bytes 786440 | tf_op jit(solution)/shard_map/ppermute | solution.py:355
  34.4 1.0 copy-start
  35.3 2.8 %copy-start.1 = (bf16[2,256,256]{2,1,0:T(8,128)(2,1)S(1)}, bf16[2,256,256]{2,1,0:T(8,128)(2,1)}, u32[]{:S(2)}) copy-start(bf16[2,256,256]{2,1,0:T(8,128)(2,1)} %get-tuple-element.22.refs_0_) | copy-start | bytes 786436
  35.4 2.7 %collective-permute-start.7 = (bf16[8,256,256]{2,1,0:T(8,128)(2,1)S(1)}, bf16[8,256,256]{2,1,0:T(8,128)(2,1)S(1)}, u32[]{:S(2)}, u32[]{:S(2)}) collective-permute-start(bf16[8,256,256]{2,1,0:T(8,128)(2,1)S(1)} %pairs.1), channel_id=1, source_target_pairs={{0,1},{1,0},{2,3},{3,2},{4,5},{5,4},{6,7},{7,6},{8,9},{9,8},{10,11... | collective-permute-start | bytes 3145736 | tf_op jit(solution)/shard_map/ppermute | solution.py:349
  75.5 2.7 %collective-permute-start.8 = (bf16[2048,256]{1,0:T(8,128)(2,1)S(1)}, bf16[2048,256]{1,0:T(8,128)(2,1)S(1)}, u32[]{:S(2)}, u32[]{:S(2)}) collective-permute-start(bf16[2048,256]{1,0:T(8,128)(2,1)S(1)} %get-tuple-element.31), channel_id=1, source_target_pairs={{0,1},{1,0},{2,3},{3,2},{4,5},{5,4},{6,7},{7,6},{8,9},{9,8},{10,11... | collective-permute-start | bytes 3145736 | tf_op jit(solution)/shard_map/ppermute | solution.py:349
  78.5 13.1 %collective-permute-start.9 = (bf16[2,256,256]{2,1,0:T(8,128)(2,1)S(1)}, bf16[2,256,256]{2,1,0:T(8,128)(2,1)S(1)}, u32[]{:S(2)}, u32[]{:S(2)}) collective-permute-start(bf16[2,256,256]{2,1,0:T(8,128)(2,1)S(1)} %get-tuple-element.33), channel_id=1, source_target_pairs={{0,12},{1,13},{2,14},{3,15},{4,8},{5,9},{6,10},{7,11},{8,4},{9,5},... | collective-permute-start | bytes 786440 | tf_op jit(solution)/shard_map/ppermute | solution.py:355
  83.2 13.9 %collective-permute-start.10 = (bf16[2,256,256]{2,1,0:T(8,128)(2,1)S(1)}, bf16[2,256,256]{2,1,0:T(8,128)(2,1)S(1)}, u32[]{:S(2)}, u32[]{:S(2)}) collective-permute-start(bf16[2,256,256]{2,1,0:T(8,128)(2,1)S(1)} %get-tuple-element.34), channel_id=1, source_target_pairs={{0,14},{1,15},{2,8},{3,9},{4,10},{5,11},{6,12},{7,13},{8,6},{9,7},... | collective-permute-start | bytes 786440 | tf_op jit(solution)/shard_map/ppermute | solution.py:355
  84.9 18.6 %collective-permute-start.11 = (bf16[2,256,256]{2,1,0:T(8,128)(2,1)S(1)}, bf16[2,256,256]{2,1,0:T(8,128)(2,1)S(1)}, u32[]{:S(2)}, u32[]{:S(2)}) collective-permute-start(bf16[2,256,256]{2,1,0:T(8,128)(2,1)S(1)} %get-tuple-element.35), channel_id=1, source_target_pairs={{0,10},{1,11},{2,12},{3,13},{4,14},{5,15},{6,8},{7,9},{8,2},{9,3},... | collective-permute-start | bytes 786440 | tf_op jit(solution)/shard_map/ppermute | solution.py:355
  87.6 20.0 %collective-permute-start.12 = (bf16[2,256,256]{2,1,0:T(8,128)(2,1)S(1)}, bf16[2,256,256]{2,1,0:T(8,128)(2,1)S(1)}, u32[]{:S(2)}, u32[]{:S(2)}) collective-permute-start(bf16[2,256,256]{2,1,0:T(8,128)(2,1)S(1)} %get-tuple-element.36), channel_id=1, source_target_pairs={{0,8},{1,9},{2,10},{3,11},{4,12},{5,13},{6,14},{7,15},{8,0},{9,1},... | collective-permute-start | bytes 786440 | tf_op jit(solution)/shard_map/ppermute | solution.py:355
  87.9 19.7 %collective-permute-start.13 = (bf16[2,256,256]{2,1,0:T(8,128)(2,1)S(1)}, bf16[2,256,256]{2,1,0:T(8,128)(2,1)S(1)}, u32[]{:S(2)}, u32[]{:S(2)}) collective-permute-start(bf16[2,256,256]{2,1,0:T(8,128)(2,1)S(1)} %get-tuple-element.37), channel_id=1, source_target_pairs={{0,4},{1,5},{2,6},{3,7},{4,0},{5,1},{6,2},{7,3},{8,12},{9,13},{10,... | collective-permute-start | bytes 786440 | tf_op jit(solution)/shard_map/ppermute | solution.py:355
  91.6 16.0 %collective-permute-start.14 = (bf16[2,256,256]{2,1,0:T(8,128)(2,1)S(1)}, bf16[2,256,256]{2,1,0:T(8,128)(2,1)S(1)}, u32[]{:S(2)}, u32[]{:S(2)}) collective-permute-start(bf16[2,256,256]{2,1,0:T(8,128)(2,1)S(1)} %get-tuple-element.38), channel_id=1, source_target_pairs={{0,6},{1,7},{2,0},{3,1},{4,2},{5,3},{6,4},{7,5},{8,14},{9,15},{10,... | collective-permute-start | bytes 786440 | tf_op jit(solution)/shard_map/ppermute | solution.py:355
  97.1 11.2 %collective-permute-start.15 = (bf16[2,256,256]{2,1,0:T(8,128)(2,1)S(1)}, bf16[2,256,256]{2,1,0:T(8,128)(2,1)S(1)}, u32[]{:S(2)}, u32[]{:S(2)}) collective-permute-start(bf16[2,256,256]{2,1,0:T(8,128)(2,1)S(1)} %get-tuple-element.39), channel_id=1, source_target_pairs={{0,2},{1,3},{2,4},{3,5},{4,6},{5,7},{6,0},{7,1},{8,10},{9,11},{10,... | collective-permute-start | bytes 786440 | tf_op jit(solution)/shard_map/ppermute | solution.py:355

commit v5 on v4

--- a/solution.py
+++ b/solution.py
@@ -20,6 +20,8 @@
 ANY = pl.BlockSpec(memory_space=pl.ANY)
 VMEM = pl.BlockSpec(memory_space=pltpu.VMEM)
 ROW = 4
+EARLY = 4
+LATE = 5
 HOPS = ((0, 0), (1, 2), (1, 1), (1, 3), (1, 0), (0, 2), (0, 1), (0, 3))
 
 
@@ -41,10 +43,11 @@
 
 
 def attention_kernel(*refs):
-    got, refs = refs[:HEADS], refs[HEADS:]
-    chunks = refs[10].shape[0]
+    got, far, refs = refs[:HEADS], refs[HEADS : HEADS + 2], refs[HEADS + 2 :]
+    far = [part.at[i] for part in far for i in range(part.shape[0])]
+    chunks = refs[9].shape[0]
     for step in range(2 * chunks):
-        attention_step(step, got, *refs)
+        attention_step(step, got, far, *refs)
 
 
 def when(condition):
@@ -56,7 +59,7 @@
 def attention_step(
     step,
     got,
-    far_ref,
+    far,
     out_ref,
     far_out_ref,
     kk_ref,
@@ -94,7 +97,7 @@
     def _():
         top = jnp.zeros((8, tokens), F32)
         for i in range(2 * blocks):
-            pair = got[i][1] if i < blocks else far_ref[i - blocks]
+            pair = got[i][1] if i < blocks else far[i - blocks][...]
             k = pair[:, 0:HEAD]
             to = slice(i * tokens, (i + 1) * tokens)
             kk_ref[to, 0:HEAD] = k
@@ -166,7 +169,7 @@
         is_far = i < half_chunks
         for j in range(per_chunk):
             block = i % half_chunks * per_chunk + j
-            pair = far_ref[block] if is_far else got[block][1]
+            pair = far[block][...] if is_far else got[block][1]
             to = slice(j * tokens, (j + 1) * tokens)
             kt_ref[:, to] = pair[:, 0:HEAD].T
             va_ref[to, 0:HEAD] = pair[:, HEAD : 2 * HEAD]
@@ -200,7 +203,7 @@
     chunks = keys // key_block
     return pl.pallas_call(
         attention_kernel,
-        in_specs=[VMEM] * (blocks + 1),
+        in_specs=[VMEM] * (blocks + 2),
         out_specs=(VMEM, VMEM),
         out_shape=(
             jax.ShapeDtypeStruct((blocks, 2, tokens, 2 * HEAD), BF16),
@@ -226,7 +229,7 @@
             transcendentals=half * keys,
         ),
         name="attention",
-    )(*got, far)
+    )(*got, *far)
 
 
 def pack_kernel(q_ref, k_ref, v_ref, g_ref, *refs):
@@ -309,11 +312,11 @@
     )(out, far)
 
 
-def unpack_kernel(*refs):
-    blocks, outs, sem = refs[:HEADS], refs[HEADS:-1], refs[-1]
+def unpack_kernel(first, count, *refs):
+    blocks, outs, sem = refs[:count], refs[-5:-1], refs[-1]
     chip = lax.axis_index("ctx") // 2
     stores = []
-    for j, hop in enumerate(HOPS):
+    for j, hop in enumerate(HOPS[first : first + count]):
         head = pl.multiple_of(chip_at(chip, hop) * HEAD, HEAD)
         for i, ref in enumerate(outs):
             store = pltpu.make_async_copy(
@@ -327,18 +330,19 @@
         store.wait()
 
 
-def unpack(blocks):
-    tokens = blocks[0].shape[1]
+def unpack(blocks, first, outs=()):
+    tokens, count = blocks[0].shape[1], len(blocks)
     whole = jax.ShapeDtypeStruct((tokens, HEADS * HEAD), BF16)
     return pl.pallas_call(
-        unpack_kernel,
-        in_specs=[VMEM] * HEADS,
+        functools.partial(unpack_kernel, first, count),
+        in_specs=[VMEM] * count + [ANY] * len(outs),
         out_specs=(ANY,) * 4,
         out_shape=(whole,) * 4,
-        scratch_shapes=[pltpu.SemaphoreType.DMA((4, HEADS))],
+        input_output_aliases={count + i: i for i in range(len(outs))},
+        scratch_shapes=[pltpu.SemaphoreType.DMA((4, count))],
         compiler_params=pltpu.CompilerParams(vmem_limit_bytes=SMALL),
         name="unpack",
-    )(*blocks)
+    )(*blocks, *outs)
 
 
 def on_device(queries, keys, values, grad_out):
@@ -356,9 +360,11 @@
         return moved
 
     got = travel(pack(queries, keys, values, grad_out), 1)
-    out, far = attention(got, other(pairs(got)))
-    attended, query_grads, key_grads, value_grads = unpack(travel(join(out, other(far)), -1))
-    return attended, query_grads, key_grads, value_grads
+    far = [other(pairs(got[:EARLY])), other(pairs(got[EARLY:]))]
+    out, far = attention(got, far)
+    back = travel(join(out, other(far)), -1)
+    outs = unpack(back[:LATE], 0)
+    return tuple(unpack(back[LATE:], LATE, outs))
 
 
 def solution(mesh):

time: 111 us -> 109 us (0.982)
  waiting for transfers between devices: 36.4 us -> 34.1 us
    ppermute x14, waiting for transfers between devices: 31.2 us -> 29.7 us  [travel(): moved.append(lax.ppermute(block, 'ctx', to))]
    ppermute x2 -> x3, waiting for transfers between devices: 5.16 us -> 4.41 us  [other(): return lax.ppermute(array, 'ctx', other_core)]
    pallas_call x2 -> x3, Pallas kernels: 38.9 us -> 39.6 us  [the longest x1 37.4 us: attention(): pl.pallas_call(attention_kernel, in_specs=[VMEM] * (blocks + 2), out_spec...]
  transfers between devices with their start and end apart: 16 -> 17, of which waited for: 12 -> 11; matrix products, arithmetic and copies ran while one was open for 0% -> 0% of each run, Pallas kernels for 0% -> 1%
where the time goes in v5:
time: 109 us; the launch traced here: 108 us
  Pallas kernels  42.5 us (39%)
  waiting for transfers between devices  34.1 us (31%)
  starting transfers between devices  29.8 us (27%)
    pallas_call x1, Pallas kernels, attention(): pl.pallas_call(attention_kernel, in_specs=[VMEM] * (blocks + 2), out_spec...  37.4 us
    ppermute x14, waiting for transfers between devices, travel(): moved.append(lax.ppermute(block, 'ctx', to))  29.7 us
    ppermute x14, starting transfers between devices, travel(): moved.append(lax.ppermute(block, 'ctx', to))  29.4 us
    ppermute x3, waiting for transfers between devices, other(): return lax.ppermute(array, 'ctx', other_core)  4.41 us
    pallas_call x1, Pallas kernels, pack(): pl.pallas_call(pack_kernel, in_specs=[ANY] * 4, out_specs=(ANY,) * HEADS,...  2.65 us
    pallas_call x2, Pallas kernels, unpack(): pl.pallas_call(functools.partial(unpack_kernel, first, count), in_specs=[...  2.21 us
  transfers between devices with their start and end apart: 17, of which 11 were waited for; matrix products, arithmetic and copies ran while one was open for 0% of the time, Pallas kernels for 1%

profile of v5, /device:TPU:0, one launch (start us, length us, event | category | flops | bytes accessed | tf_op | source)
XLA Modules:
  0.0 108.3 jit_solution(13811470530073082330)
XLA Ops:
  0.6 2.6 %pack.1 = (bf16[2,256,256]{2,1,0:T(8,128)(2,1)}, bf16[2,256,256]{2,1,0:T(8,128)(2,1)}, bf16[2,256,256]{2,1,0:T(8,128)(2,1)}, bf16[2,256,256]{2,1,0:T(8,128)(2,1)...) custom-call(bf16[256,1024]{1,0:T(8,128)(2,1)} %q_ref.1, ...), custom_call_target="tpu_custom_call" | custom-call | tf_op jit(solution)/shard_map/pack/pallas_call | solution.py:262
  3.3 6.5 %collective-permute-start = (bf16[2,256,256]{2,1,0:T(8,128)(2,1)}, bf16[2,256,256]{2,1,0:T(8,128)(2,1)S(1)}, u32[]{:S(2)}, u32[]{:S(2)}) collective-permute-start(bf16[2,256,256]{2,1,0:T(8,128)(2,1)} %get-tuple-element.27), channel_id=1, source_target_pairs={{0,12},{1,13},{2,14},{3,15},{4,8},{5,9},{6,10},{7,11},{8,4},{9,5},... | collective-permute-start | bytes 786440 | tf_op jit(solution)/shard_map/ppermute | solution.py:359
  9.8 1.0 collective-permute-start.1
  10.7 4.7 %collective-permute-start.2 = (bf16[2,256,256]{2,1,0:T(8,128)(2,1)}, bf16[2,256,256]{2,1,0:T(8,128)(2,1)S(1)}, u32[]{:S(2)}, u32[]{:S(2)}) collective-permute-start(bf16[2,256,256]{2,1,0:T(8,128)(2,1)} %get-tuple-element.29), channel_id=1, source_target_pairs={{0,14},{1,15},{2,8},{3,9},{4,10},{5,11},{6,12},{7,13},{8,6},{9,7},... | collective-permute-start | bytes 786440 | tf_op jit(solution)/shard_map/ppermute | solution.py:359
  15.4 0.5 collective-permute-start.3
  15.9 1.2 %collective-permute-done.refs_1_ = bf16[2,256,256]{2,1,0:T(8,128)(2,1)S(1)} collective-permute-done((bf16[2,256,256]{2,1,0:T(8,128)(2,1)}, bf16[2,256,256]{2,1,0:T(8,128)(2,1)S(1)}, u32[]{:S(2)}, u32[]{:S(2)}) %collective-permute-start) | collective-permute-done | bytes 262176 | tf_op jit(solution)/shard_map/ppermute | solution.py:359
  17.1 1.2 %collective-permute-start.5 = (bf16[2,256,256]{2,1,0:T(8,128)(2,1)}, bf16[2,256,256]{2,1,0:T(8,128)(2,1)S(1)}, u32[]{:S(2)}, u32[]{:S(2)}) collective-permute-start(bf16[2,256,256]{2,1,0:T(8,128)(2,1)} %get-tuple-element.32), channel_id=1, source_target_pairs={{0,2},{1,3},{2,4},{3,5},{4,6},{5,7},{6,0},{7,1},{8,10},{9,11},{10,... | collective-permute-start | bytes 786440 | tf_op jit(solution)/shard_map/ppermute | solution.py:359
  18.4 5.2 %collective-permute-done.1.refs_2_ = bf16[2,256,256]{2,1,0:T(8,128)(2,1)S(1)} collective-permute-done((bf16[2,256,256]{2,1,0:T(8,128)(2,1)}, bf16[2,256,256]{2,1,0:T(8,128)(2,1)S(1)}, u32[]{:S(2)}, u32[]{:S(2)}) %collective-permute-start.1) | collective-permute-done | bytes 262176 | tf_op jit(solution)/shard_map/ppermute | solution.py:359
  23.6 6.3 %collective-permute-done.2.refs_3_ = bf16[2,256,256]{2,1,0:T(8,128)(2,1)S(1)} collective-permute-done((bf16[2,256,256]{2,1,0:T(8,128)(2,1)}, bf16[2,256,256]{2,1,0:T(8,128)(2,1)S(1)}, u32[]{:S(2)}, u32[]{:S(2)}) %collective-permute-start.2) | collective-permute-done | bytes 262176 | tf_op jit(solution)/shard_map/ppermute | solution.py:359
  30.0 0.9 copy-done
  30.9 0.1 collective-permute-start.7
  31.0 3.2 %collective-permute-done.3.refs_0_.refs_4_ = bf16[2,256,256]{2,1,0:T(8,128)(2,1)S(1)} collective-permute-done((bf16[2,256,256]{2,1,0:T(8,128)(2,1)}, bf16[2,256,256]{2,1,0:T(8,128)(2,1)S(1)}, u32[]{:S(2)}, u32[]{:S(2)}) %collective-permute-start.3) | collective-permute-done | bytes 262176 | tf_op jit(solution)/shard_map/ppermute | solution.py:359
  34.3 0.1 collective-permute-done.6.refs_3_.refs_7_
  34.4 0.1 collective-permute-start.8
  34.5 1.9 %collective-permute-done.8.refs_9_ = bf16[4,256,256]{2,1,0:T(8,128)(2,1)S(1)} collective-permute-done((bf16[4,256,256]{2,1,0:T(8,128)(2,1)S(1)}, bf16[4,256,256]{2,1,0:T(8,128)(2,1)S(1)}, u32[]{:S(2)}, u32[]{:S(2)}) %collective-permute-start.8) | collective-permute-done | bytes 524320 | tf_op jit(solution)/shard_map/ppermute | solution.py:353
  36.4 37.4 %attention.1 = (bf16[8,2,256,256]{3,2,1,0:T(8,128)(2,1)S(1)}, bf16[2048,256]{1,0:T(8,128)(2,1)S(1)}) custom-call(bf16[2,256,256]{2,1,0:T(8,128)(2,1)S(1)} %copy-done.1, bf16[2,256,256]{2,1,0:T(8,128)(2,1)S(1)} %collective-permute-done.refs_1_, bf16[2,256,256]{2,1,0:T(8,128)(2,1)S(1)} %collective-permute-done.1.refs_2_, ...), custom_call_target="tpu_custom_call" | custom-call | flops 12884901888 | bytes 3145728 | tf_op jit(solution)/shard_map/attention/pallas_call | solution.py:204
  73.8 0.2 collective-permute-start.9
  74.0 2.5 %collective-permute-done.9.far_ref = bf16[2048,256]{1,0:T(8,128)(2,1)S(1)} collective-permute-done((bf16[2048,256]{1,0:T(8,128)(2,1)S(1)}, bf16[2048,256]{1,0:T(8,128)(2,1)S(1)}, u32[]{:S(2)}, u32[]{:S(2)}) %collective-permute-start.9) | collective-permute-done | bytes 1048608 | tf_op jit(solution)/shard_map/ppermute | solution.py:353
  76.5 0.2 join.1
  76.8 4.7 %collective-permute-start.13 = (bf16[2,256,256]{2,1,0:T(8,128)(2,1)S(1)}, bf16[2,256,256]{2,1,0:T(8,128)(2,1)S(1)}, u32[]{:S(2)}, u32[]{:S(2)}) collective-permute-start(bf16[2,256,256]{2,1,0:T(8,128)(2,1)S(1)} %get-tuple-element.40), channel_id=1, source_target_pairs={{0,12},{1,13},{2,14},{3,15},{4,8},{5,9},{6,10},{7,11},{8,4},{9,5},... | collective-permute-start | bytes 786440 | tf_op jit(solution)/shard_map/ppermute | solution.py:359
  81.5 1.7 %collective-permute-start.14 = (bf16[2,256,256]{2,1,0:T(8,128)(2,1)S(1)}, bf16[2,256,256]{2,1,0:T(8,128)(2,1)S(1)}, u32[]{:S(2)}, u32[]{:S(2)}) collective-permute-start(bf16[2,256,256]{2,1,0:T(8,128)(2,1)S(1)} %get-tuple-element.41), channel_id=1, source_target_pairs={{0,14},{1,15},{2,8},{3,9},{4,10},{5,11},{6,12},{7,13},{8,6},{9,7},... | collective-permute-start | bytes 786440 | tf_op jit(solution)/shard_map/ppermute | solution.py:359
  83.2 1.5 %collective-permute-start.10 = (bf16[2,256,256]{2,1,0:T(8,128)(2,1)S(1)}, bf16[2,256,256]{2,1,0:T(8,128)(2,1)S(1)}, u32[]{:S(2)}, u32[]{:S(2)}) collective-permute-start(bf16[2,256,256]{2,1,0:T(8,128)(2,1)S(1)} %get-tuple-element.36), channel_id=1, source_target_pairs={{0,4},{1,5},{2,6},{3,7},{4,0},{5,1},{6,2},{7,3},{8,12},{9,13},{10,... | collective-permute-start | bytes 786440 | tf_op jit(solution)/shard_map/ppermute | solution.py:359
  84.7 2.0 %collective-permute-start.15 = (bf16[2,256,256]{2,1,0:T(8,128)(2,1)S(1)}, bf16[2,256,256]{2,1,0:T(8,128)(2,1)S(1)}, u32[]{:S(2)}, u32[]{:S(2)}) collective-permute-start(bf16[2,256,256]{2,1,0:T(8,128)(2,1)S(1)} %get-tuple-element.42), channel_id=1, source_target_pairs={{0,10},{1,11},{2,12},{3,13},{4,14},{5,15},{6,8},{7,9},{8,2},{9,3},... | collective-permute-start | bytes 786440 | tf_op jit(solution)/shard_map/ppermute | solution.py:359
  86.7 0.6 collective-permute-start.16
  87.3 2.6 %collective-permute-done.13.refs_1_ = bf16[2,256,256]{2,1,0:T(8,128)(2,1)S(1)} collective-permute-done((bf16[2,256,256]{2,1,0:T(8,128)(2,1)S(1)}, bf16[2,256,256]{2,1,0:T(8,128)(2,1)S(1)}, u32[]{:S(2)}, u32[]{:S(2)}) %collective-permute-start.13) | collective-permute-done | bytes 262176 | tf_op jit(solution)/shard_map/ppermute | solution.py:359
  89.9 3.5 %collective-permute-start.11 = (bf16[2,256,256]{2,1,0:T(8,128)(2,1)S(1)}, bf16[2,256,256]{2,1,0:T(8,128)(2,1)S(1)}, u32[]{:S(2)}, u32[]{:S(2)}) collective-permute-start(bf16[2,256,256]{2,1,0:T(8,128)(2,1)S(1)} %get-tuple-element.37), channel_id=1, source_target_pairs={{0,6},{1,7},{2,0},{3,1},{4,2},{5,3},{6,4},{7,5},{8,14},{9,15},{10,... | collective-permute-start | bytes 786440 | tf_op jit(solution)/shard_map/ppermute | solution.py:359
  93.4 2.0 %collective-permute-done.14.refs_2_ = bf16[2,256,256]{2,1,0:T(8,128)(2,1)S(1)} collective-permute-done((bf16[2,256,256]{2,1,0:T(8,128)(2,1)S(1)}, bf16[2,256,256]{2,1,0:T(8,128)(2,1)S(1)}, u32[]{:S(2)}, u32[]{:S(2)}) %collective-permute-start.14) | collective-permute-done | bytes 262176 | tf_op jit(solution)/shard_map/ppermute | solution.py:359
  95.4 1.5 %collective-permute-start.12 = (bf16[2,256,256]{2,1,0:T(8,128)(2,1)S(1)}, bf16[2,256,256]{2,1,0:T(8,128)(2,1)S(1)}, u32[]{:S(2)}, u32[]{:S(2)}) collective-permute-start(bf16[2,256,256]{2,1,0:T(8,128)(2,1)S(1)} %get-tuple-element.38), channel_id=1, source_target_pairs={{0,2},{1,3},{2,4},{3,5},{4,6},{5,7},{6,0},{7,1},{8,10},{9,11},{10,... | collective-permute-start | bytes 786440 | tf_op jit(solution)/shard_map/ppermute | solution.py:359
  96.9 4.8 %collective-permute-done.15.refs_3_ = bf16[2,256,256]{2,1,0:T(8,128)(2,1)S(1)} collective-permute-done((bf16[2,256,256]{2,1,0:T(8,128)(2,1)S(1)}, bf16[2,256,256]{2,1,0:T(8,128)(2,1)S(1)}, u32[]{:S(2)}, u32[]{:S(2)}) %collective-permute-start.15) | collective-permute-done | bytes 262176 | tf_op jit(solution)/shard_map/ppermute | solution.py:359
  101.7 4.2 %collective-permute-done.16.refs_4_ = bf16[2,256,256]{2,1,0:T(8,128)(2,1)S(1)} collective-permute-done((bf16[2,256,256]{2,1,0:T(8,128)(2,1)S(1)}, bf16[2,256,256]{2,1,0:T(8,128)(2,1)S(1)}, u32[]{:S(2)}, u32[]{:S(2)}) %collective-permute-start.16) | collective-permute-done | bytes 262176 | tf_op jit(solution)/shard_map/ppermute | solution.py:359
  105.9 1.2 %unpack.2 = (bf16[256,1024]{1,0:T(8,128)(2,1)}, bf16[256,1024]{1,0:T(8,128)(2,1)}, bf16[256,1024]{1,0:T(8,128)(2,1)}, bf16[256,1024]{1,0:T(8,128)(2,1)}) custom-call(bf16[2,256,256]{2,1,0:T(8,128)(2,1)S(1)} %get-tuple-element.39.refs_0_, bf16[2,256,256]{2,1,0:T(8,128)(2,1)S(1)} %collective-permute-done.13.refs_1_, ...), custom_call_target="tpu_custom_call" | custom-call | tf_op jit(solution)/shard_map/unpack/pallas_call | solution.py:336
  107.1 1.0 unpack.3
  (13 shorter events, 0.1 us)
Async XLA Ops:
  3.3 13.8 %collective-permute-start = (bf16[2,256,256]{2,1,0:T(8,128)(2,1)}, bf16[2,256,256]{2,1,0:T(8,128)(2,1)S(1)}, u32[]{:S(2)}, u32[]{:S(2)}) collective-permute-start(bf16[2,256,256]{2,1,0:T(8,128)(2,1)} %get-tuple-element.27), channel_id=1, source_target_pairs={{0,12},{1,13},{2,14},{3,15},{4,8},{5,9},{6,10},{7,11},{8,4},{9,5},... | collective-permute-start | bytes 786440 | tf_op jit(solution)/shard_map/ppermute | solution.py:359
  9.8 13.8 %collective-permute-start.1 = (bf16[2,256,256]{2,1,0:T(8,128)(2,1)}, bf16[2,256,256]{2,1,0:T(8,128)(2,1)S(1)}, u32[]{:S(2)}, u32[]{:S(2)}) collective-permute-start(bf16[2,256,256]{2,1,0:T(8,128)(2,1)} %get-tuple-element.28), channel_id=1, source_target_pairs={{0,10},{1,11},{2,12},{3,13},{4,14},{5,15},{6,8},{7,9},{8,2},{9,3},... | collective-permute-start | bytes 786440 | tf_op jit(solution)/shard_map/ppermute | solution.py:359
  10.7 19.2 %collective-permute-start.2 = (bf16[2,256,256]{2,1,0:T(8,128)(2,1)}, bf16[2,256,256]{2,1,0:T(8,128)(2,1)S(1)}, u32[]{:S(2)}, u32[]{:S(2)}) collective-permute-start(bf16[2,256,256]{2,1,0:T(8,128)(2,1)} %get-tuple-element.29), channel_id=1, source_target_pairs={{0,14},{1,15},{2,8},{3,9},{4,10},{5,11},{6,12},{7,13},{8,6},{9,7},... | collective-permute-start | bytes 786440 | tf_op jit(solution)/shard_map/ppermute | solution.py:359
  15.4 18.8 %collective-permute-start.3 = (bf16[2,256,256]{2,1,0:T(8,128)(2,1)}, bf16[2,256,256]{2,1,0:T(8,128)(2,1)S(1)}, u32[]{:S(2)}, u32[]{:S(2)}) collective-permute-start(bf16[2,256,256]{2,1,0:T(8,128)(2,1)} %get-tuple-element.30), channel_id=1, source_target_pairs={{0,8},{1,9},{2,10},{3,11},{4,12},{5,13},{6,14},{7,15},{8,0},{9,1},... | collective-permute-start | bytes 786440 | tf_op jit(solution)/shard_map/ppermute | solution.py:359
  15.9 18.3 %collective-permute-start.4 = (bf16[2,256,256]{2,1,0:T(8,128)(2,1)}, bf16[2,256,256]{2,1,0:T(8,128)(2,1)S(1)}, u32[]{:S(2)}, u32[]{:S(2)}) collective-permute-start(bf16[2,256,256]{2,1,0:T(8,128)(2,1)} %get-tuple-element.31), channel_id=1, source_target_pairs={{0,4},{1,5},{2,6},{3,7},{4,0},{5,1},{6,2},{7,3},{8,12},{9,13},{10,... | collective-permute-start | bytes 786440 | tf_op jit(solution)/shard_map/ppermute | solution.py:359
  17.1 17.1 %collective-permute-start.5 = (bf16[2,256,256]{2,1,0:T(8,128)(2,1)}, bf16[2,256,256]{2,1,0:T(8,128)(2,1)S(1)}, u32[]{:S(2)}, u32[]{:S(2)}) collective-permute-start(bf16[2,256,256]{2,1,0:T(8,128)(2,1)} %get-tuple-element.32), channel_id=1, source_target_pairs={{0,2},{1,3},{2,4},{3,5},{4,6},{5,7},{6,0},{7,1},{8,10},{9,11},{10,... | collective-permute-start | bytes 786440 | tf_op jit(solution)/shard_map/ppermute | solution.py:359
  23.6 10.8 %collective-permute-start.6 = (bf16[2,256,256]{2,1,0:T(8,128)(2,1)}, bf16[2,256,256]{2,1,0:T(8,128)(2,1)S(1)}, u32[]{:S(2)}, u32[]{:S(2)}) collective-permute-start(bf16[2,256,256]{2,1,0:T(8,128)(2,1)} %get-tuple-element.33), channel_id=1, source_target_pairs={{0,6},{1,7},{2,0},{3,1},{4,2},{5,3},{6,4},{7,5},{8,14},{9,15},{10,... | collective-permute-start | bytes 786440 | tf_op jit(solution)/shard_map/ppermute | solution.py:359
  30.0 1.0 copy-start
  30.9 5.5 %copy-start.1 = (bf16[2,256,256]{2,1,0:T(8,128)(2,1)S(1)}, bf16[2,256,256]{2,1,0:T(8,128)(2,1)}, u32[]{:S(2)}) copy-start(bf16[2,256,256]{2,1,0:T(8,128)(2,1)} %get-tuple-element.26.refs_0_) | copy-start | bytes 786436
  30.9 3.6 %collective-permute-start.7 = (bf16[4,256,256]{2,1,0:T(8,128)(2,1)S(1)}, bf16[4,256,256]{2,1,0:T(8,128)(2,1)S(1)}, u32[]{:S(2)}, u32[]{:S(2)}) collective-permute-start(bf16[4,256,256]{2,1,0:T(8,128)(2,1)S(1)} %pairs.2), channel_id=1, source_target_pairs={{0,1},{1,0},{2,3},{3,2},{4,5},{5,4},{6,7},{7,6},{8,9},{9,8},{10,11... | collective-permute-start | bytes 1572872 | tf_op jit(solution)/shard_map/ppermute | solution.py:353
  34.4 2.0 %collective-permute-start.8 = (bf16[4,256,256]{2,1,0:T(8,128)(2,1)S(1)}, bf16[4,256,256]{2,1,0:T(8,128)(2,1)S(1)}, u32[]{:S(2)}, u32[]{:S(2)}) collective-permute-start(bf16[4,256,256]{2,1,0:T(8,128)(2,1)S(1)} %pairs.3), channel_id=1, source_target_pairs={{0,1},{1,0},{2,3},{3,2},{4,5},{5,4},{6,7},{7,6},{8,9},{9,8},{10,11... | collective-permute-start | bytes 1572872 | tf_op jit(solution)/shard_map/ppermute | solution.py:353
  73.8 2.7 %collective-permute-start.9 = (bf16[2048,256]{1,0:T(8,128)(2,1)S(1)}, bf16[2048,256]{1,0:T(8,128)(2,1)S(1)}, u32[]{:S(2)}, u32[]{:S(2)}) collective-permute-start(bf16[2048,256]{1,0:T(8,128)(2,1)S(1)} %get-tuple-element.35), channel_id=1, source_target_pairs={{0,1},{1,0},{2,3},{3,2},{4,5},{5,4},{6,7},{7,6},{8,9},{9,8},{10,11... | collective-permute-start | bytes 3145736 | tf_op jit(solution)/shard_map/ppermute | solution.py:353
  76.8 13.1 %collective-permute-start.13 = (bf16[2,256,256]{2,1,0:T(8,128)(2,1)S(1)}, bf16[2,256,256]{2,1,0:T(8,128)(2,1)S(1)}, u32[]{:S(2)}, u32[]{:S(2)}) collective-permute-start(bf16[2,256,256]{2,1,0:T(8,128)(2,1)S(1)} %get-tuple-element.40), channel_id=1, source_target_pairs={{0,12},{1,13},{2,14},{3,15},{4,8},{5,9},{6,10},{7,11},{8,4},{9,5},... | collective-permute-start | bytes 786440 | tf_op jit(solution)/shard_map/ppermute | solution.py:359
  81.5 13.9 %collective-permute-start.14 = (bf16[2,256,256]{2,1,0:T(8,128)(2,1)S(1)}, bf16[2,256,256]{2,1,0:T(8,128)(2,1)S(1)}, u32[]{:S(2)}, u32[]{:S(2)}) collective-permute-start(bf16[2,256,256]{2,1,0:T(8,128)(2,1)S(1)} %get-tuple-element.41), channel_id=1, source_target_pairs={{0,14},{1,15},{2,8},{3,9},{4,10},{5,11},{6,12},{7,13},{8,6},{9,7},... | collective-permute-start | bytes 786440 | tf_op jit(solution)/shard_map/ppermute | solution.py:359
  83.2 23.9 %collective-permute-start.10 = (bf16[2,256,256]{2,1,0:T(8,128)(2,1)S(1)}, bf16[2,256,256]{2,1,0:T(8,128)(2,1)S(1)}, u32[]{:S(2)}, u32[]{:S(2)}) collective-permute-start(bf16[2,256,256]{2,1,0:T(8,128)(2,1)S(1)} %get-tuple-element.36), channel_id=1, source_target_pairs={{0,4},{1,5},{2,6},{3,7},{4,0},{5,1},{6,2},{7,3},{8,12},{9,13},{10,... | collective-permute-start | bytes 786440 | tf_op jit(solution)/shard_map/ppermute | solution.py:359
  84.7 17.0 %collective-permute-start.15 = (bf16[2,256,256]{2,1,0:T(8,128)(2,1)S(1)}, bf16[2,256,256]{2,1,0:T(8,128)(2,1)S(1)}, u32[]{:S(2)}, u32[]{:S(2)}) collective-permute-start(bf16[2,256,256]{2,1,0:T(8,128)(2,1)S(1)} %get-tuple-element.42), channel_id=1, source_target_pairs={{0,10},{1,11},{2,12},{3,13},{4,14},{5,15},{6,8},{7,9},{8,2},{9,3},... | collective-permute-start | bytes 786440 | tf_op jit(solution)/shard_map/ppermute | solution.py:359
  86.7 19.2 %collective-permute-start.16 = (bf16[2,256,256]{2,1,0:T(8,128)(2,1)S(1)}, bf16[2,256,256]{2,1,0:T(8,128)(2,1)S(1)}, u32[]{:S(2)}, u32[]{:S(2)}) collective-permute-start(bf16[2,256,256]{2,1,0:T(8,128)(2,1)S(1)} %get-tuple-element.43), channel_id=1, source_target_pairs={{0,8},{1,9},{2,10},{3,11},{4,12},{5,13},{6,14},{7,15},{8,0},{9,1},... | collective-permute-start | bytes 786440 | tf_op jit(solution)/shard_map/ppermute | solution.py:359
  89.9 17.2 %collective-permute-start.11 = (bf16[2,256,256]{2,1,0:T(8,128)(2,1)S(1)}, bf16[2,256,256]{2,1,0:T(8,128)(2,1)S(1)}, u32[]{:S(2)}, u32[]{:S(2)}) collective-permute-start(bf16[2,256,256]{2,1,0:T(8,128)(2,1)S(1)} %get-tuple-element.37), channel_id=1, source_target_pairs={{0,6},{1,7},{2,0},{3,1},{4,2},{5,3},{6,4},{7,5},{8,14},{9,15},{10,... | collective-permute-start | bytes 786440 | tf_op jit(solution)/shard_map/ppermute | solution.py:359
  95.4 11.7 %collective-permute-start.12 = (bf16[2,256,256]{2,1,0:T(8,128)(2,1)S(1)}, bf16[2,256,256]{2,1,0:T(8,128)(2,1)S(1)}, u32[]{:S(2)}, u32[]{:S(2)}) collective-permute-start(bf16[2,256,256]{2,1,0:T(8,128)(2,1)S(1)} %get-tuple-element.38), channel_id=1, source_target_pairs={{0,2},{1,3},{2,4},{3,5},{4,6},{5,7},{6,0},{7,1},{8,10},{9,11},{10,... | collective-permute-start | bytes 786440 | tf_op jit(solution)/shard_map/ppermute | solution.py:359

commit v6 on v5

--- a/solution.py
+++ b/solution.py
@@ -45,9 +45,10 @@
 def attention_kernel(*refs):
     got, far, refs = refs[:HEADS], refs[HEADS : HEADS + 2], refs[HEADS + 2 :]
     far = [part.at[i] for part in far for i in range(part.shape[0])]
-    chunks = refs[9].shape[0]
+    out, far_outs, refs = refs[0], refs[1:3], refs[3:]
+    chunks = refs[7].shape[0]
     for step in range(2 * chunks):
-        attention_step(step, got, far, *refs)
+        attention_step(step, got, far, out, far_outs, *refs)
 
 
 def when(condition):
@@ -61,7 +62,7 @@
     got,
     far,
     out_ref,
-    far_out_ref,
+    far_outs,
     kk_ref,
     vt_ref,
     kt_ref,
@@ -181,8 +182,8 @@
         total_ref[0:HEAD, :] += dot(kt_ref[...], g, NN)
 
         if is_far:
-            far_out_ref[span(i), 0:HEAD] = dk
-            far_out_ref[span(i), HEAD : 2 * HEAD] = dv
+            far_outs[i][:, 0:HEAD] = dk
+            far_outs[i][:, HEAD : 2 * HEAD] = dv
         else:
             to = slice((i - half_chunks) * per_chunk, (i - half_chunks + 1) * per_chunk)
             out_ref[to, 1, :, 0:HEAD] = dk.reshape(per_chunk, tokens, HEAD)
@@ -204,10 +205,10 @@
     return pl.pallas_call(
         attention_kernel,
         in_specs=[VMEM] * (blocks + 2),
-        out_specs=(VMEM, VMEM),
+        out_specs=(VMEM,) * 3,
         out_shape=(
             jax.ShapeDtypeStruct((blocks, 2, tokens, 2 * HEAD), BF16),
-            jax.ShapeDtypeStruct((half, 2 * HEAD), BF16),
+            *[jax.ShapeDtypeStruct((key_block, 2 * HEAD), BF16)] * (half // key_block),
         ),
         scratch_shapes=[
             pltpu.VMEM((keys, 2 * HEAD), BF16),
@@ -291,19 +292,19 @@
     )(*blocks)
 
 
-def join_kernel(in_ref, far_ref, *outs):
+def join_kernel(first, in_ref, far_ref, *outs):
     tokens = in_ref.shape[2]
     for i, out_ref in enumerate(outs):
-        out_ref[0] = in_ref[i, 0]
-        near = in_ref[i, 1].astype(F32)
+        out_ref[0] = in_ref[first + i, 0]
+        near = in_ref[first + i, 1].astype(F32)
         far = far_ref[i * tokens : (i + 1) * tokens, :].astype(F32)
         out_ref[1] = (near + far).astype(BF16)
 
 
-def join(out, far):
-    blocks = out.shape[0]
-    return pl.pallas_call(
-        join_kernel,
+def join(out, far, first):
+    blocks = far.shape[0] // out.shape[2]
+    return pl.pallas_call(
+        functools.partial(join_kernel, first),
         in_specs=[VMEM] * 2,
         out_specs=(VMEM,) * blocks,
         out_shape=(jax.ShapeDtypeStruct(out.shape[1:], BF16),) * blocks,
@@ -361,8 +362,9 @@
 
     got = travel(pack(queries, keys, values, grad_out), 1)
     far = [other(pairs(got[:EARLY])), other(pairs(got[EARLY:]))]
-    out, far = attention(got, far)
-    back = travel(join(out, other(far)), -1)
+    out, *far = attention(got, far)
+    joined = [join(out, other(part), i * HEADS // len(far)) for i, part in enumerate(far)]
+    back = travel([*joined[0], *joined[1]], -1)
     outs = unpack(back[:LATE], 0)
     return tuple(unpack(back[LATE:], LATE, outs))
 

time: 109 us -> 109 us (level)
  starting transfers between devices: 29.8 us -> 32.7 us
  waiting for transfers between devices: 34.1 us -> 31.9 us
    ppermute x14, starting transfers between devices: 29.4 us -> 31.9 us  [travel(): moved.append(lax.ppermute(block, 'ctx', to))]
    ppermute x3 -> x4, waiting for transfers between devices: 4.41 us -> 3.29 us  [other(): return lax.ppermute(array, 'ctx', other_core)]
    ppermute x14, waiting for transfers between devices: 29.7 us -> 28.6 us  [travel(): moved.append(lax.ppermute(block, 'ctx', to))]
  transfers between devices with their start and end apart: 17 -> 18, of which waited for: 11 -> 12; matrix products, arithmetic and copies ran while one was open for 0% -> 0% of each run, Pallas kernels for 1% -> 1%
where the time goes in v6:
time: 109 us
  Pallas kernels  42.5 us (39%)
  starting transfers between devices  32.7 us (30%)
  waiting for transfers between devices  31.9 us (29%)
    pallas_call x1, Pallas kernels, attention(): pl.pallas_call(attention_kernel, in_specs=[VMEM] * (blocks + 2), out_spec...  37.4 us
    ppermute x14, starting transfers between devices, travel(): moved.append(lax.ppermute(block, 'ctx', to))  31.9 us
    ppermute x14, waiting for transfers between devices, travel(): moved.append(lax.ppermute(block, 'ctx', to))  28.6 us
    ppermute x4, waiting for transfers between devices, other(): return lax.ppermute(array, 'ctx', other_core)  3.29 us
    pallas_call x1, Pallas kernels, pack(): pl.pallas_call(pack_kernel, in_specs=[ANY] * 4, out_specs=(ANY,) * HEADS,...  2.65 us
  transfers between devices with their start and end apart: 18, of which 12 were waited for; matrix products, arithmetic and copies ran while one was open for 0% of the time, Pallas kernels for 1%

profile of v6, /device:TPU:0, one launch (start us, length us, event | category | flops | bytes accessed | tf_op | source)
XLA Modules:
  0.0 108.9 jit_solution(7830571752717084986)
XLA Ops:
  0.6 2.7 %pack.1 = (bf16[2,256,256]{2,1,0:T(8,128)(2,1)}, bf16[2,256,256]{2,1,0:T(8,128)(2,1)}, bf16[2,256,256]{2,1,0:T(8,128)(2,1)}, bf16[2,256,256]{2,1,0:T(8,128)(2,1)...) custom-call(bf16[256,1024]{1,0:T(8,128)(2,1)} %q_ref.1, ...), custom_call_target="tpu_custom_call" | custom-call | tf_op jit(solution)/shard_map/pack/pallas_call | solution.py:263
  3.3 6.5 %collective-permute-start = (bf16[2,256,256]{2,1,0:T(8,128)(2,1)}, bf16[2,256,256]{2,1,0:T(8,128)(2,1)S(1)}, u32[]{:S(2)}, u32[]{:S(2)}) collective-permute-start(bf16[2,256,256]{2,1,0:T(8,128)(2,1)} %get-tuple-element.28), channel_id=1, source_target_pairs={{0,12},{1,13},{2,14},{3,15},{4,8},{5,9},{6,10},{7,11},{8,4},{9,5},... | collective-permute-start | bytes 786440 | tf_op jit(solution)/shard_map/ppermute | solution.py:360
  9.8 1.0 collective-permute-start.1
  10.8 4.7 %collective-permute-start.2 = (bf16[2,256,256]{2,1,0:T(8,128)(2,1)}, bf16[2,256,256]{2,1,0:T(8,128)(2,1)S(1)}, u32[]{:S(2)}, u32[]{:S(2)}) collective-permute-start(bf16[2,256,256]{2,1,0:T(8,128)(2,1)} %get-tuple-element.30), channel_id=1, source_target_pairs={{0,14},{1,15},{2,8},{3,9},{4,10},{5,11},{6,12},{7,13},{8,6},{9,7},... | collective-permute-start | bytes 786440 | tf_op jit(solution)/shard_map/ppermute | solution.py:360
  15.4 0.5 collective-permute-start.3
  15.9 1.2 %collective-permute-done.refs_1_ = bf16[2,256,256]{2,1,0:T(8,128)(2,1)S(1)} collective-permute-done((bf16[2,256,256]{2,1,0:T(8,128)(2,1)}, bf16[2,256,256]{2,1,0:T(8,128)(2,1)S(1)}, u32[]{:S(2)}, u32[]{:S(2)}) %collective-permute-start) | collective-permute-done | bytes 262176 | tf_op jit(solution)/shard_map/ppermute | solution.py:360
  17.1 1.2 %collective-permute-start.5 = (bf16[2,256,256]{2,1,0:T(8,128)(2,1)}, bf16[2,256,256]{2,1,0:T(8,128)(2,1)S(1)}, u32[]{:S(2)}, u32[]{:S(2)}) collective-permute-start(bf16[2,256,256]{2,1,0:T(8,128)(2,1)} %get-tuple-element.33), channel_id=1, source_target_pairs={{0,2},{1,3},{2,4},{3,5},{4,6},{5,7},{6,0},{7,1},{8,10},{9,11},{10,... | collective-permute-start | bytes 786440 | tf_op jit(solution)/shard_map/ppermute | solution.py:360
  18.4 5.2 %collective-permute-done.1.refs_2_ = bf16[2,256,256]{2,1,0:T(8,128)(2,1)S(1)} collective-permute-done((bf16[2,256,256]{2,1,0:T(8,128)(2,1)}, bf16[2,256,256]{2,1,0:T(8,128)(2,1)S(1)}, u32[]{:S(2)}, u32[]{:S(2)}) %collective-permute-start.1) | collective-permute-done | bytes 262176 | tf_op jit(solution)/shard_map/ppermute | solution.py:360
  23.6 6.3 %collective-permute-done.2.refs_3_ = bf16[2,256,256]{2,1,0:T(8,128)(2,1)S(1)} collective-permute-done((bf16[2,256,256]{2,1,0:T(8,128)(2,1)}, bf16[2,256,256]{2,1,0:T(8,128)(2,1)S(1)}, u32[]{:S(2)}, u32[]{:S(2)}) %collective-permute-start.2) | collective-permute-done | bytes 262176 | tf_op jit(solution)/shard_map/ppermute | solution.py:360
  30.0 0.9 copy-done
  31.0 3.2 %collective-permute-done.3.refs_0_.refs_4_ = bf16[2,256,256]{2,1,0:T(8,128)(2,1)S(1)} collective-permute-done((bf16[2,256,256]{2,1,0:T(8,128)(2,1)}, bf16[2,256,256]{2,1,0:T(8,128)(2,1)S(1)}, u32[]{:S(2)}, u32[]{:S(2)}) %collective-permute-start.3) | collective-permute-done | bytes 262176 | tf_op jit(solution)/shard_map/ppermute | solution.py:360
  34.3 0.1 collective-permute-done.6.refs_3_.refs_7_
  34.5 1.9 %collective-permute-done.8.refs_9_ = bf16[4,256,256]{2,1,0:T(8,128)(2,1)S(1)} collective-permute-done((bf16[4,256,256]{2,1,0:T(8,128)(2,1)S(1)}, bf16[4,256,256]{2,1,0:T(8,128)(2,1)S(1)}, u32[]{:S(2)}, u32[]{:S(2)}) %collective-permute-start.8) | collective-permute-done | bytes 524320 | tf_op jit(solution)/shard_map/ppermute | solution.py:354
  36.4 37.4 %attention.1 = (bf16[8,2,256,256]{3,2,1,0:T(8,128)(2,1)S(1)}, bf16[1024,256]{1,0:T(8,128)(2,1)S(1)}, bf16[1024,256]{1,0:T(8,128)(2,1)S(1)}) custom-call(bf16[2,256,256]{2,1,0:T(8,128)(2,1)S(1)} %copy-done.1, bf16[2,256,256]{2,1,0:T(8,128)(2,1)S(1)} %collective-permute-done.refs_1_, bf16[2,256,256]{2,1,0:T(8,128)(2,1)S(1)} %collective-permute-done.1.refs_2_, ...), custom_call_target="tpu_custom_call" | custom-call | flops 12884901888 | bytes 3145728 | tf_op jit(solution)/shard_map/attention/pallas_call | solution.py:205
  73.8 0.2 collective-permute-start.9
  74.0 0.4 collective-permute-start.13
  74.4 1.4 %collective-permute-done.9.far_ref = bf16[1024,256]{1,0:T(8,128)(2,1)S(1)} collective-permute-done((bf16[1024,256]{1,0:T(8,128)(2,1)S(1)}, bf16[1024,256]{1,0:T(8,128)(2,1)S(1)}, u32[]{:S(2)}, u32[]{:S(2)}) %collective-permute-start.9) | collective-permute-done | bytes 524320 | tf_op jit(solution)/shard_map/ppermute | solution.py:354
  75.8 0.1 join.2
  75.9 3.1 %collective-permute-start.17 = (bf16[2,256,256]{2,1,0:T(8,128)(2,1)S(1)}, bf16[2,256,256]{2,1,0:T(8,128)(2,1)S(1)}, u32[]{:S(2)}, u32[]{:S(2)}) collective-permute-start(bf16[2,256,256]{2,1,0:T(8,128)(2,1)S(1)} %get-tuple-element.45), channel_id=1, source_target_pairs={{0,8},{1,9},{2,10},{3,11},{4,12},{5,13},{6,14},{7,15},{8,0},{9,1},... | collective-permute-start | bytes 786440 | tf_op jit(solution)/shard_map/ppermute | solution.py:360
  79.1 0.1 join.3
  79.2 2.2 %collective-permute-start.14 = (bf16[2,256,256]{2,1,0:T(8,128)(2,1)S(1)}, bf16[2,256,256]{2,1,0:T(8,128)(2,1)S(1)}, u32[]{:S(2)}, u32[]{:S(2)}) collective-permute-start(bf16[2,256,256]{2,1,0:T(8,128)(2,1)S(1)} %get-tuple-element.42), channel_id=1, source_target_pairs={{0,12},{1,13},{2,14},{3,15},{4,8},{5,9},{6,10},{7,11},{8,4},{9,5},... | collective-permute-start | bytes 786440 | tf_op jit(solution)/shard_map/ppermute | solution.py:360
  81.4 1.4 %collective-permute-start.10 = (bf16[2,256,256]{2,1,0:T(8,128)(2,1)S(1)}, bf16[2,256,256]{2,1,0:T(8,128)(2,1)S(1)}, u32[]{:S(2)}, u32[]{:S(2)}) collective-permute-start(bf16[2,256,256]{2,1,0:T(8,128)(2,1)S(1)} %get-tuple-element.37), channel_id=1, source_target_pairs={{0,4},{1,5},{2,6},{3,7},{4,0},{5,1},{6,2},{7,3},{8,12},{9,13},{10,... | collective-permute-start | bytes 786440 | tf_op jit(solution)/shard_map/ppermute | solution.py:360
  82.8 4.5 %collective-permute-start.15 = (bf16[2,256,256]{2,1,0:T(8,128)(2,1)S(1)}, bf16[2,256,256]{2,1,0:T(8,128)(2,1)S(1)}, u32[]{:S(2)}, u32[]{:S(2)}) collective-permute-start(bf16[2,256,256]{2,1,0:T(8,128)(2,1)S(1)} %get-tuple-element.43), channel_id=1, source_target_pairs={{0,14},{1,15},{2,8},{3,9},{4,10},{5,11},{6,12},{7,13},{8,6},{9,7},... | collective-permute-start | bytes 786440 | tf_op jit(solution)/shard_map/ppermute | solution.py:360
  87.3 3.6 %collective-permute-start.11 = (bf16[2,256,256]{2,1,0:T(8,128)(2,1)S(1)}, bf16[2,256,256]{2,1,0:T(8,128)(2,1)S(1)}, u32[]{:S(2)}, u32[]{:S(2)}) collective-permute-start(bf16[2,256,256]{2,1,0:T(8,128)(2,1)S(1)} %get-tuple-element.38), channel_id=1, source_target_pairs={{0,6},{1,7},{2,0},{3,1},{4,2},{5,3},{6,4},{7,5},{8,14},{9,15},{10,... | collective-permute-start | bytes 786440 | tf_op jit(solution)/shard_map/ppermute | solution.py:360
  90.9 2.8 %collective-permute-done.14.refs_1_ = bf16[2,256,256]{2,1,0:T(8,128)(2,1)S(1)} collective-permute-done((bf16[2,256,256]{2,1,0:T(8,128)(2,1)S(1)}, bf16[2,256,256]{2,1,0:T(8,128)(2,1)S(1)}, u32[]{:S(2)}, u32[]{:S(2)}) %collective-permute-start.14) | collective-permute-done | bytes 262176 | tf_op jit(solution)/shard_map/ppermute | solution.py:360
  93.7 3.2 %collective-permute-start.12 = (bf16[2,256,256]{2,1,0:T(8,128)(2,1)S(1)}, bf16[2,256,256]{2,1,0:T(8,128)(2,1)S(1)}, u32[]{:S(2)}, u32[]{:S(2)}) collective-permute-start(bf16[2,256,256]{2,1,0:T(8,128)(2,1)S(1)} %get-tuple-element.39), channel_id=1, source_target_pairs={{0,2},{1,3},{2,4},{3,5},{4,6},{5,7},{6,0},{7,1},{8,10},{9,11},{10,... | collective-permute-start | bytes 786440 | tf_op jit(solution)/shard_map/ppermute | solution.py:360
  96.9 1.7 %collective-permute-done.15.refs_2_ = bf16[2,256,256]{2,1,0:T(8,128)(2,1)S(1)} collective-permute-done((bf16[2,256,256]{2,1,0:T(8,128)(2,1)S(1)}, bf16[2,256,256]{2,1,0:T(8,128)(2,1)S(1)}, u32[]{:S(2)}, u32[]{:S(2)}) %collective-permute-start.15) | collective-permute-done | bytes 262176 | tf_op jit(solution)/shard_map/ppermute | solution.py:360
  98.6 6.5 %collective-permute-done.16.refs_3_ = bf16[2,256,256]{2,1,0:T(8,128)(2,1)S(1)} collective-permute-done((bf16[2,256,256]{2,1,0:T(8,128)(2,1)S(1)}, bf16[2,256,256]{2,1,0:T(8,128)(2,1)S(1)}, u32[]{:S(2)}, u32[]{:S(2)}) %collective-permute-start.16) | collective-permute-done | bytes 262176 | tf_op jit(solution)/shard_map/ppermute | solution.py:360
  105.1 1.2 %unpack.2 = (bf16[256,1024]{1,0:T(8,128)(2,1)}, bf16[256,1024]{1,0:T(8,128)(2,1)}, bf16[256,1024]{1,0:T(8,128)(2,1)}, bf16[256,1024]{1,0:T(8,128)(2,1)}) custom-call(bf16[2,256,256]{2,1,0:T(8,128)(2,1)S(1)} %get-tuple-element.41.refs_0_, bf16[2,256,256]{2,1,0:T(8,128)(2,1)S(1)} %collective-permute-done.14.refs_1_, ...), custom_call_target="tpu_custom_call" | custom-call | tf_op jit(solution)/shard_map/unpack/pallas_call | solution.py:337
  106.3 0.6 collective-permute-done.11.refs_1_
  106.9 0.9 collective-permute-done.12.refs_2_
  107.8 1.0 unpack.3
  (16 shorter events, 0.3 us)
Async XLA Ops:
  3.3 13.8 %collective-permute-start = (bf16[2,256,256]{2,1,0:T(8,128)(2,1)}, bf16[2,256,256]{2,1,0:T(8,128)(2,1)S(1)}, u32[]{:S(2)}, u32[]{:S(2)}) collective-permute-start(bf16[2,256,256]{2,1,0:T(8,128)(2,1)} %get-tuple-element.28), channel_id=1, source_target_pairs={{0,12},{1,13},{2,14},{3,15},{4,8},{5,9},{6,10},{7,11},{8,4},{9,5},... | collective-permute-start | bytes 786440 | tf_op jit(solution)/shard_map/ppermute | solution.py:360
  9.8 13.8 %collective-permute-start.1 = (bf16[2,256,256]{2,1,0:T(8,128)(2,1)}, bf16[2,256,256]{2,1,0:T(8,128)(2,1)S(1)}, u32[]{:S(2)}, u32[]{:S(2)}) collective-permute-start(bf16[2,256,256]{2,1,0:T(8,128)(2,1)} %get-tuple-element.29), channel_id=1, source_target_pairs={{0,10},{1,11},{2,12},{3,13},{4,14},{5,15},{6,8},{7,9},{8,2},{9,3},... | collective-permute-start | bytes 786440 | tf_op jit(solution)/shard_map/ppermute | solution.py:360
  10.8 19.2 %collective-permute-start.2 = (bf16[2,256,256]{2,1,0:T(8,128)(2,1)}, bf16[2,256,256]{2,1,0:T(8,128)(2,1)S(1)}, u32[]{:S(2)}, u32[]{:S(2)}) collective-permute-start(bf16[2,256,256]{2,1,0:T(8,128)(2,1)} %get-tuple-element.30), channel_id=1, source_target_pairs={{0,14},{1,15},{2,8},{3,9},{4,10},{5,11},{6,12},{7,13},{8,6},{9,7},... | collective-permute-start | bytes 786440 | tf_op jit(solution)/shard_map/ppermute | solution.py:360
  15.4 18.8 %collective-permute-start.3 = (bf16[2,256,256]{2,1,0:T(8,128)(2,1)}, bf16[2,256,256]{2,1,0:T(8,128)(2,1)S(1)}, u32[]{:S(2)}, u32[]{:S(2)}) collective-permute-start(bf16[2,256,256]{2,1,0:T(8,128)(2,1)} %get-tuple-element.31), channel_id=1, source_target_pairs={{0,8},{1,9},{2,10},{3,11},{4,12},{5,13},{6,14},{7,15},{8,0},{9,1},... | collective-permute-start | bytes 786440 | tf_op jit(solution)/shard_map/ppermute | solution.py:360
  15.9 18.3 %collective-permute-start.4 = (bf16[2,256,256]{2,1,0:T(8,128)(2,1)}, bf16[2,256,256]{2,1,0:T(8,128)(2,1)S(1)}, u32[]{:S(2)}, u32[]{:S(2)}) collective-permute-start(bf16[2,256,256]{2,1,0:T(8,128)(2,1)} %get-tuple-element.32), channel_id=1, source_target_pairs={{0,4},{1,5},{2,6},{3,7},{4,0},{5,1},{6,2},{7,3},{8,12},{9,13},{10,... | collective-permute-start | bytes 786440 | tf_op jit(solution)/shard_map/ppermute | solution.py:360
  17.1 17.1 %collective-permute-start.5 = (bf16[2,256,256]{2,1,0:T(8,128)(2,1)}, bf16[2,256,256]{2,1,0:T(8,128)(2,1)S(1)}, u32[]{:S(2)}, u32[]{:S(2)}) collective-permute-start(bf16[2,256,256]{2,1,0:T(8,128)(2,1)} %get-tuple-element.33), channel_id=1, source_target_pairs={{0,2},{1,3},{2,4},{3,5},{4,6},{5,7},{6,0},{7,1},{8,10},{9,11},{10,... | collective-permute-start | bytes 786440 | tf_op jit(solution)/shard_map/ppermute | solution.py:360
  23.6 10.8 %collective-permute-start.6 = (bf16[2,256,256]{2,1,0:T(8,128)(2,1)}, bf16[2,256,256]{2,1,0:T(8,128)(2,1)S(1)}, u32[]{:S(2)}, u32[]{:S(2)}) collective-permute-start(bf16[2,256,256]{2,1,0:T(8,128)(2,1)} %get-tuple-element.34), channel_id=1, source_target_pairs={{0,6},{1,7},{2,0},{3,1},{4,2},{5,3},{6,4},{7,5},{8,14},{9,15},{10,... | collective-permute-start | bytes 786440 | tf_op jit(solution)/shard_map/ppermute | solution.py:360
  30.0 1.0 copy-start
  30.9 5.5 %copy-start.1 = (bf16[2,256,256]{2,1,0:T(8,128)(2,1)S(1)}, bf16[2,256,256]{2,1,0:T(8,128)(2,1)}, u32[]{:S(2)}) copy-start(bf16[2,256,256]{2,1,0:T(8,128)(2,1)} %get-tuple-element.27.refs_0_) | copy-start | bytes 786436
  31.0 3.6 %collective-permute-start.7 = (bf16[4,256,256]{2,1,0:T(8,128)(2,1)S(1)}, bf16[4,256,256]{2,1,0:T(8,128)(2,1)S(1)}, u32[]{:S(2)}, u32[]{:S(2)}) collective-permute-start(bf16[4,256,256]{2,1,0:T(8,128)(2,1)S(1)} %pairs.2), channel_id=1, source_target_pairs={{0,1},{1,0},{2,3},{3,2},{4,5},{5,4},{6,7},{7,6},{8,9},{9,8},{10,11... | collective-permute-start | bytes 1572872 | tf_op jit(solution)/shard_map/ppermute | solution.py:354
  34.4 2.0 %collective-permute-start.8 = (bf16[4,256,256]{2,1,0:T(8,128)(2,1)S(1)}, bf16[4,256,256]{2,1,0:T(8,128)(2,1)S(1)}, u32[]{:S(2)}, u32[]{:S(2)}) collective-permute-start(bf16[4,256,256]{2,1,0:T(8,128)(2,1)S(1)} %pairs.3), channel_id=1, source_target_pairs={{0,1},{1,0},{2,3},{3,2},{4,5},{5,4},{6,7},{7,6},{8,9},{9,8},{10,11... | collective-permute-start | bytes 1572872 | tf_op jit(solution)/shard_map/ppermute | solution.py:354
  73.8 2.0 %collective-permute-start.9 = (bf16[1024,256]{1,0:T(8,128)(2,1)S(1)}, bf16[1024,256]{1,0:T(8,128)(2,1)S(1)}, u32[]{:S(2)}, u32[]{:S(2)}) collective-permute-start(bf16[1024,256]{1,0:T(8,128)(2,1)S(1)} %get-tuple-element.36), channel_id=1, source_target_pairs={{0,1},{1,0},{2,3},{3,2},{4,5},{5,4},{6,7},{7,6},{8,9},{9,8},{10,11... | collective-permute-start | bytes 1572872 | tf_op jit(solution)/shard_map/ppermute | solution.py:354
  74.0 5.1 %collective-permute-start.13 = (bf16[1024,256]{1,0:T(8,128)(2,1)S(1)}, bf16[1024,256]{1,0:T(8,128)(2,1)S(1)}, u32[]{:S(2)}, u32[]{:S(2)}) collective-permute-start(bf16[1024,256]{1,0:T(8,128)(2,1)S(1)} %get-tuple-element.40), channel_id=1, source_target_pairs={{0,1},{1,0},{2,3},{3,2},{4,5},{5,4},{6,7},{7,6},{8,9},{9,8},{10,11... | collective-permute-start | bytes 1572872 | tf_op jit(solution)/shard_map/ppermute | solution.py:354
  75.9 11.4 %collective-permute-start.17 = (bf16[2,256,256]{2,1,0:T(8,128)(2,1)S(1)}, bf16[2,256,256]{2,1,0:T(8,128)(2,1)S(1)}, u32[]{:S(2)}, u32[]{:S(2)}) collective-permute-start(bf16[2,256,256]{2,1,0:T(8,128)(2,1)S(1)} %get-tuple-element.45), channel_id=1, source_target_pairs={{0,8},{1,9},{2,10},{3,11},{4,12},{5,13},{6,14},{7,15},{8,0},{9,1},... | collective-permute-start | bytes 786440 | tf_op jit(solution)/shard_map/ppermute | solution.py:360
  79.2 14.5 %collective-permute-start.14 = (bf16[2,256,256]{2,1,0:T(8,128)(2,1)S(1)}, bf16[2,256,256]{2,1,0:T(8,128)(2,1)S(1)}, u32[]{:S(2)}, u32[]{:S(2)}) collective-permute-start(bf16[2,256,256]{2,1,0:T(8,128)(2,1)S(1)} %get-tuple-element.42), channel_id=1, source_target_pairs={{0,12},{1,13},{2,14},{3,15},{4,8},{5,9},{6,10},{7,11},{8,4},{9,5},... | collective-permute-start | bytes 786440 | tf_op jit(solution)/shard_map/ppermute | solution.py:360
  81.4 25.0 %collective-permute-start.10 = (bf16[2,256,256]{2,1,0:T(8,128)(2,1)S(1)}, bf16[2,256,256]{2,1,0:T(8,128)(2,1)S(1)}, u32[]{:S(2)}, u32[]{:S(2)}) collective-permute-start(bf16[2,256,256]{2,1,0:T(8,128)(2,1)S(1)} %get-tuple-element.37), channel_id=1, source_target_pairs={{0,4},{1,5},{2,6},{3,7},{4,0},{5,1},{6,2},{7,3},{8,12},{9,13},{10,... | collective-permute-start | bytes 786440 | tf_op jit(solution)/shard_map/ppermute | solution.py:360
  82.8 15.8 %collective-permute-start.15 = (bf16[2,256,256]{2,1,0:T(8,128)(2,1)S(1)}, bf16[2,256,256]{2,1,0:T(8,128)(2,1)S(1)}, u32[]{:S(2)}, u32[]{:S(2)}) collective-permute-start(bf16[2,256,256]{2,1,0:T(8,128)(2,1)S(1)} %get-tuple-element.43), channel_id=1, source_target_pairs={{0,14},{1,15},{2,8},{3,9},{4,10},{5,11},{6,12},{7,13},{8,6},{9,7},... | collective-permute-start | bytes 786440 | tf_op jit(solution)/shard_map/ppermute | solution.py:360
  87.3 17.8 %collective-permute-start.16 = (bf16[2,256,256]{2,1,0:T(8,128)(2,1)S(1)}, bf16[2,256,256]{2,1,0:T(8,128)(2,1)S(1)}, u32[]{:S(2)}, u32[]{:S(2)}) collective-permute-start(bf16[2,256,256]{2,1,0:T(8,128)(2,1)S(1)} %get-tuple-element.44), channel_id=1, source_target_pairs={{0,10},{1,11},{2,12},{3,13},{4,14},{5,15},{6,8},{7,9},{8,2},{9,3},... | collective-permute-start | bytes 786440 | tf_op jit(solution)/shard_map/ppermute | solution.py:360
  87.3 19.6 %collective-permute-start.11 = (bf16[2,256,256]{2,1,0:T(8,128)(2,1)S(1)}, bf16[2,256,256]{2,1,0:T(8,128)(2,1)S(1)}, u32[]{:S(2)}, u32[]{:S(2)}) collective-permute-start(bf16[2,256,256]{2,1,0:T(8,128)(2,1)S(1)} %get-tuple-element.38), channel_id=1, source_target_pairs={{0,6},{1,7},{2,0},{3,1},{4,2},{5,3},{6,4},{7,5},{8,14},{9,15},{10,... | collective-permute-start | bytes 786440 | tf_op jit(solution)/shard_map/ppermute | solution.py:360
  93.7 14.1 %collective-permute-start.12 = (bf16[2,256,256]{2,1,0:T(8,128)(2,1)S(1)}, bf16[2,256,256]{2,1,0:T(8,128)(2,1)S(1)}, u32[]{:S(2)}, u32[]{:S(2)}) collective-permute-start(bf16[2,256,256]{2,1,0:T(8,128)(2,1)S(1)} %get-tuple-element.39), channel_id=1, source_target_pairs={{0,2},{1,3},{2,4},{3,5},{4,6},{5,7},{6,0},{7,1},{8,10},{9,11},{10,... | collective-permute-start | bytes 786440 | tf_op jit(solution)/shard_map/ppermute | solution.py:360
